TPU v7x, 32 devices: a whole 2x2x4 slice. The times are simulated.
32 devices in a mesh: dp: 16 (over z, y, core), mp: 2 (over x).
Axes of the slice: x: 2, y: 2, z: 4, core: 2. Of those that a mesh axis runs over, the one named last changes fastest.
Arguments:
- patches: bfloat16 [16, 1568, 768], P('dp', 'mp'), may hold values from -6 to 6
- cube_mask: int32 [16, 1568], P('dp', 'mp'), may hold values from 0 to 1, as said below
- mask_token: float32 [768], replicated, may hold values from -5 to 5
- cotangent: bfloat16 [16, 1568, 768], P('dp', 'mp'), may hold values from -6 to 6
- vectors: float32 [12, 768], replicated
- vector_first: float32 [12, 768], replicated
- vector_second: float32 [12, 768], replicated, as said below
- attend_master: float32 [768, 3, 768], P('dp', None, 'mp')
- attend_first: float32 [768, 3, 768], P('dp', None, 'mp')
- attend_second: float32 [768, 3, 768], P('dp', None, 'mp'), as said below
- mixing_master: float32 [768, 768], P('dp', 'mp')
- mixing_first: float32 [768, 768], P('dp', 'mp')
- mixing_second: float32 [768, 768], P('dp', 'mp'), as said below
- expand_master: float32 [768, 3072], P('dp', 'mp')
- expand_first: float32 [768, 3072], P('dp', 'mp')
- expand_second: float32 [768, 3072], P('dp', 'mp'), as said below
- shrink_master: float32 [768, 3072], P('dp', 'mp')
- shrink_first: float32 [768, 3072], P('dp', 'mp')
- shrink_second: float32 [768, 3072], P('dp', 'mp'), as said below
Outputs:
- block_out: bfloat16 [16, 1568, 768], P('dp', 'mp')
- patch_grad: bfloat16 [16, 1568, 768], P('dp', 'mp')
- token_grad: float32 [768], replicated
- bias_grad: float32 [768], replicated
- attend_moment: float32 [768, 3, 768], P('dp', None, 'mp')
- attend_square: float32 [768, 3, 768], P('dp', None, 'mp')
- attend_weight: float32 [768, 3, 768], P('dp', None, 'mp')
- attend_copy: bfloat16 [768, 3, 768], P('dp', None, 'mp')
- mixing_moment: float32 [768, 768], P('dp', 'mp')
- mixing_square: float32 [768, 768], P('dp', 'mp')
- mixing_weight: float32 [768, 768], P('dp', 'mp')
- mixing_copy: bfloat16 [768, 768], P('dp', 'mp')
- expand_moment: float32 [768, 3072], P('dp', 'mp')
- expand_square: float32 [768, 3072], P('dp', 'mp')
- expand_weight: float32 [768, 3072], P('dp', 'mp')
- expand_copy: bfloat16 [768, 3072], P('dp', 'mp')
- shrink_moment: float32 [768, 3072], P('dp', 'mp')
- shrink_square: float32 [768, 3072], P('dp', 'mp')
- shrink_weight: float32 [768, 3072], P('dp', 'mp')
- shrink_copy: bfloat16 [768, 3072], P('dp', 'mp')
- vector_moment: float32 [12, 768], replicated
- vector_square: float32 [12, 768], replicated
- vector_weight: float32 [12, 768], replicated
- trust_norms: float32 [4, 2], replicated
Inputs may be any that keep to these rules, and one draw needn't show every extreme that they name: `cube_mask`: 1 marks a masked tube; masked tubes come in whole cubes of 2 x 2 x 2 tubes of a clip's 8 x 14 x 14 grid, tubes ordered by time, height, width. `attend_second`: positive. `mixing_second`: positive. `expand_second`: positive. `shrink_second`: positive. `vector_second`: positive.
All inputs are finite; a program needn't handle non-finite values.
Results may differ from a plain program's by a relative error of at most 0.018.
The roundings to bfloat16 on the way count: a program that leaves them out, or rounds other values in their place, can miss the bound.
Values may be sent and summed in bfloat16 or wider, within the bound.
A program may use at most 128 MiB of HBM per device.

v0:
```python
import jax
import jax.numpy as jnp
from jax import lax
from jax.sharding import PartitionSpec as P

HD = 64
QBLK = 784
STEP = 5


def layer_norm(values, scales, shifts):
    centered = values - jnp.mean(values, axis=-1, keepdims=True)
    spread = jnp.mean(centered * centered, axis=-1, keepdims=True)
    return centered * lax.rsqrt(spread + 1e-06) * scales + shifts


def gelu_exact(inputs):
    return jax.nn.gelu(inputs, approximate=False)


def to_heads(flat_rows, clip_count, length, width):
    head_count = width // HD
    shaped = flat_rows.reshape(clip_count, length, head_count, HD).transpose(0, 2, 1, 3)
    return shaped.reshape(clip_count * head_count, length, HD)


def from_heads(stacked, clip_count, length, width):
    head_count = width // HD
    shaped = stacked.reshape(clip_count, head_count, length, HD).transpose(0, 2, 1, 3)
    return shaped.reshape(clip_count * length, width)


def head_forward(triple):
    queries, key_rows, values = triple

    def one_block(block_rows):
        scores = jnp.einsum(
            "qd,kd->qk", block_rows, key_rows, preferred_element_type=jnp.float32
        ) * HD ** (-0.5)
        row_max = jnp.max(scores, axis=-1, keepdims=True)
        weights = jnp.exp(scores - row_max)
        row_total = jnp.sum(weights, axis=-1, keepdims=True)
        attention = (weights / row_total).astype(jnp.bfloat16)
        result = jnp.dot(attention, values, preferred_element_type=jnp.float32)
        return (result, (row_max + jnp.log(row_total))[:, 0])

    result, log_total = lax.map(one_block, queries.reshape(-1, QBLK, HD))
    return (result.reshape(-1, HD), log_total.reshape(-1))


def head_backward(items):
    queries, key_rows, values, grad_out, log_total = items

    def one_block(carried, pieces):
        grad_keys, grad_values = carried
        block_rows, grad_rows, block_total = pieces
        scores = jnp.einsum(
            "qd,kd->qk", block_rows, key_rows, preferred_element_type=jnp.float32
        ) * HD ** (-0.5)
        attention = jnp.exp(scores - block_total[:, None])
        grad_attention = jnp.einsum(
            "qd,kd->qk", grad_rows, values, preferred_element_type=jnp.float32
        )
        row_dot = jnp.sum(attention * grad_attention, axis=-1, keepdims=True)
        grad_scores = (attention * (grad_attention - row_dot)).astype(jnp.bfloat16)
        grad_block = jnp.dot(grad_scores, key_rows, preferred_element_type=jnp.float32) * HD ** (
            -0.5
        )
        grad_keys = grad_keys + jnp.einsum(
            "qk,qd->kd", grad_scores, block_rows, preferred_element_type=jnp.float32
        ) * HD ** (-0.5)
        grad_values = grad_values + jnp.einsum(
            "qk,qd->kd",
            attention.astype(jnp.bfloat16),
            grad_rows,
            preferred_element_type=jnp.float32,
        )
        return ((grad_keys, grad_values), grad_block)

    empty_rows = jnp.zeros(key_rows.shape, jnp.float32)
    (grad_keys, grad_values), grad_queries = lax.scan(
        one_block,
        (empty_rows, empty_rows),
        (
            queries.reshape(-1, QBLK, HD),
            grad_out.reshape(-1, QBLK, HD),
            log_total.reshape(-1, QBLK),
        ),
    )
    return (grad_queries.reshape(-1, HD), grad_keys, grad_values)


def lamb_terms(weight, moment, square, gradient):
    moment_new = 0.5 * moment + 0.5 * gradient
    square_new = 0.5 * square + 0.5 * gradient * gradient
    correct = 1.0 - 0.5**STEP
    update = moment_new / correct / (jnp.sqrt(square_new / correct) + 1e-06) + 0.01 * weight
    return (
        moment_new,
        square_new,
        update,
        jnp.stack([jnp.sum(weight * weight), jnp.sum(update * update)]),
    )


def lamb_apply(weight, update, norms):
    renewed = weight - 0.5 * norms[0] / (norms[1] + 1e-06) * update
    return (renewed, renewed.astype(jnp.bfloat16))


def per_device(
    patches,
    cube_mask,
    mask_token,
    cotangent,
    vectors,
    vector_first,
    vector_second,
    attend_master,
    attend_first,
    attend_second,
    mixing_master,
    mixing_first,
    mixing_second,
    expand_master,
    expand_first,
    expand_second,
    shrink_master,
    shrink_first,
    shrink_second,
):
    clip_count, half_rows, width = patches.shape
    position = lax.axis_index("mp")
    length = half_rows * lax.axis_size("mp")
    total_rows = clip_count * length
    attend_w, mixing_w, expand_w, shrink_w = (
        lax.all_gather(attend_master.astype(jnp.bfloat16), "dp", axis=0, tiled=True),
        lax.all_gather(mixing_master.astype(jnp.bfloat16), "dp", axis=0, tiled=True),
        lax.all_gather(expand_master.astype(jnp.bfloat16), "dp", axis=0, tiled=True),
        lax.all_gather(shrink_master.astype(jnp.bfloat16), "dp", axis=0, tiled=True),
    )
    local_width = attend_w.shape[2]
    hidden_local = expand_w.shape[1]
    attend_flat = attend_w.reshape(width, 3 * local_width)
    query_bias = lax.dynamic_slice_in_dim(vectors[2], position * local_width, local_width)
    value_bias = lax.dynamic_slice_in_dim(vectors[3], position * local_width, local_width)
    up_bias = lax.dynamic_slice_in_dim(
        vectors[7:11].reshape(-1), position * hidden_local, hidden_local
    )
    chosen = cube_mask[:, :, None] > 0
    residual = jnp.where(chosen, mask_token, patches.astype(jnp.float32))
    normed = layer_norm(residual, vectors[0], vectors[1]).astype(jnp.bfloat16)
    first_rows = lax.all_gather(normed, "mp", axis=1, tiled=True).reshape(total_rows, width)
    joined = jnp.dot(first_rows, attend_flat, preferred_element_type=jnp.float32)
    queries = (joined[:, :local_width] + query_bias).astype(jnp.bfloat16)
    key_rows = joined[:, local_width : 2 * local_width].astype(jnp.bfloat16)
    values = (joined[:, 2 * local_width :] + value_bias).astype(jnp.bfloat16)
    query_heads = to_heads(queries, clip_count, length, local_width)
    key_heads = to_heads(key_rows, clip_count, length, local_width)
    value_heads = to_heads(values, clip_count, length, local_width)
    head_out, log_total = lax.map(head_forward, (query_heads, key_heads, value_heads))
    mixed = from_heads(head_out, clip_count, length, local_width).astype(jnp.bfloat16)
    pieces = jnp.einsum("rc,dc->rd", mixed, mixing_w, preferred_element_type=jnp.float32).reshape(
        clip_count, length, width
    )
    branch = (
        lax.psum_scatter(pieces.astype(jnp.bfloat16), "mp", scatter_dimension=1, tiled=True).astype(
            jnp.float32
        )
        + vectors[4]
    )
    middle = residual + branch
    normed_two = layer_norm(middle, vectors[5], vectors[6]).astype(jnp.bfloat16)
    second_rows = lax.all_gather(normed_two, "mp", axis=1, tiled=True).reshape(total_rows, width)
    hidden = jnp.dot(second_rows, expand_w, preferred_element_type=jnp.float32) + up_bias
    active = gelu_exact(hidden).astype(jnp.bfloat16)
    pieces_two = jnp.einsum(
        "rf,df->rd", active, shrink_w, preferred_element_type=jnp.float32
    ).reshape(clip_count, length, width)
    branch_two = (
        lax.psum_scatter(
            pieces_two.astype(jnp.bfloat16), "mp", scatter_dimension=1, tiled=True
        ).astype(jnp.float32)
        + vectors[11]
    )
    block_out = (middle + branch_two).astype(jnp.bfloat16)
    grad_top = cotangent.astype(jnp.float32)
    top_rows = lax.all_gather(cotangent, "mp", axis=1, tiled=True).reshape(total_rows, width)
    shrink_grad = jnp.einsum("rd,rf->df", top_rows, active, preferred_element_type=jnp.float32)
    grad_active = jnp.dot(top_rows, shrink_w, preferred_element_type=jnp.float32)
    unused_value, gelu_back = jax.vjp(gelu_exact, hidden)
    grad_hidden = gelu_back(grad_active)[0].astype(jnp.bfloat16)
    expand_grad = jnp.einsum(
        "rd,rf->df", second_rows, grad_hidden, preferred_element_type=jnp.float32
    )
    up_grad = jnp.sum(grad_hidden.astype(jnp.float32), axis=0)
    grad_norm_two = jnp.einsum(
        "rf,df->rd", grad_hidden, expand_w, preferred_element_type=jnp.float32
    ).reshape(clip_count, length, width)
    grad_norm_two = lax.psum_scatter(
        grad_norm_two.astype(jnp.bfloat16), "mp", scatter_dimension=1, tiled=True
    ).astype(jnp.float32)
    unused_norm, norm_back = jax.vjp(layer_norm, middle, vectors[5], vectors[6])
    grad_middle, gain_two_grad, shift_two_grad = norm_back(grad_norm_two)
    grad_middle = grad_middle + grad_top
    grad_middle_low = grad_middle.astype(jnp.bfloat16)
    middle_rows = lax.all_gather(grad_middle_low, "mp", axis=1, tiled=True).reshape(
        total_rows, width
    )
    mixing_grad = jnp.einsum("rd,rc->dc", middle_rows, mixed, preferred_element_type=jnp.float32)
    grad_mixed = jnp.dot(middle_rows, mixing_w, preferred_element_type=jnp.float32).astype(
        jnp.bfloat16
    )
    grad_heads = to_heads(grad_mixed, clip_count, length, local_width)
    grad_query_heads, grad_key_heads, grad_value_heads = lax.map(
        head_backward, (query_heads, key_heads, value_heads, grad_heads, log_total)
    )
    grad_queries = from_heads(grad_query_heads, clip_count, length, local_width).astype(
        jnp.bfloat16
    )
    grad_keys = from_heads(grad_key_heads, clip_count, length, local_width).astype(jnp.bfloat16)
    grad_values = from_heads(grad_value_heads, clip_count, length, local_width).astype(jnp.bfloat16)
    grad_joined = jnp.concatenate([grad_queries, grad_keys, grad_values], axis=1)
    attend_grad = jnp.einsum(
        "rd,rc->dc", first_rows, grad_joined, preferred_element_type=jnp.float32
    ).reshape(width, 3, local_width)
    attend_total, mixing_total, expand_total, shrink_total = (
        lax.psum_scatter(attend_grad, "dp", scatter_dimension=0, tiled=True),
        lax.psum_scatter(mixing_grad, "dp", scatter_dimension=0, tiled=True),
        lax.psum_scatter(expand_grad, "dp", scatter_dimension=0, tiled=True),
        lax.psum_scatter(shrink_grad, "dp", scatter_dimension=0, tiled=True),
    )
    grad_norm_one = jnp.einsum(
        "rc,dc->rd", grad_joined, attend_flat, preferred_element_type=jnp.float32
    ).reshape(clip_count, length, width)
    grad_norm_one = lax.psum_scatter(
        grad_norm_one.astype(jnp.bfloat16), "mp", scatter_dimension=1, tiled=True
    ).astype(jnp.float32)
    unused_first, norm_back_one = jax.vjp(layer_norm, residual, vectors[0], vectors[1])
    grad_start, gain_one_grad, shift_one_grad = norm_back_one(grad_norm_one)
    grad_start = grad_start + grad_middle
    patch_grad = jnp.where(chosen, 0.0, grad_start).astype(jnp.bfloat16)
    token_part = jnp.sum(jnp.where(chosen, grad_start, 0.0), axis=(0, 1))
    empty_width = jnp.zeros((width,), jnp.float32)
    query_full = lax.dynamic_update_slice_in_dim(
        empty_width, jnp.sum(grad_queries.astype(jnp.float32), axis=0), position * local_width, 0
    )
    value_full = lax.dynamic_update_slice_in_dim(
        empty_width, jnp.sum(grad_values.astype(jnp.float32), axis=0), position * local_width, 0
    )
    up_full = lax.dynamic_update_slice_in_dim(
        jnp.zeros((4 * width,), jnp.float32), up_grad, position * hidden_local, 0
    ).reshape(4, width)
    mixing_bias_grad = jnp.sum(grad_middle_low.astype(jnp.float32), axis=(0, 1))
    output_bias_grad = jnp.sum(grad_top, axis=(0, 1))
    vector_part = jnp.concatenate(
        [
            jnp.stack(
                [
                    gain_one_grad,
                    shift_one_grad,
                    query_full,
                    value_full,
                    mixing_bias_grad,
                    gain_two_grad,
                    shift_two_grad,
                ]
            ),
            up_full,
            output_bias_grad[None, :],
        ],
        axis=0,
    )
    attend_terms = lamb_terms(attend_master, attend_first, attend_second, attend_total)
    mixing_terms = lamb_terms(mixing_master, mixing_first, mixing_second, mixing_total)
    expand_terms = lamb_terms(expand_master, expand_first, expand_second, expand_total)
    shrink_terms = lamb_terms(shrink_master, shrink_first, shrink_second, shrink_total)
    squares = jnp.stack([attend_terms[3], mixing_terms[3], expand_terms[3], shrink_terms[3]])
    vector_total, token_grad, square_total = lax.psum(
        (vector_part, token_part, squares), ("dp", "mp")
    )
    trust_norms = jnp.sqrt(square_total)
    attend_weight, attend_copy = lamb_apply(attend_master, attend_terms[2], trust_norms[0])
    mixing_weight, mixing_copy = lamb_apply(mixing_master, mixing_terms[2], trust_norms[1])
    expand_weight, expand_copy = lamb_apply(expand_master, expand_terms[2], trust_norms[2])
    shrink_weight, shrink_copy = lamb_apply(shrink_master, shrink_terms[2], trust_norms[3])
    vector_moment = 0.5 * vector_first + 0.5 * vector_total
    vector_square = 0.5 * vector_second + 0.5 * vector_total * vector_total
    correct = 1.0 - 0.5**STEP
    vector_update = (
        vector_moment / correct / (jnp.sqrt(vector_square / correct) + 1e-06) + 0.01 * vectors
    )
    row_weight = jnp.sqrt(jnp.sum(vectors * vectors, axis=-1, keepdims=True))
    row_update = jnp.sqrt(jnp.sum(vector_update * vector_update, axis=-1, keepdims=True))
    vector_weight = vectors - 0.5 * row_weight / (row_update + 1e-06) * vector_update
    bias_grad = vector_total[11]
    return (
        block_out,
        patch_grad,
        token_grad,
        bias_grad,
        attend_terms[0],
        attend_terms[1],
        attend_weight,
        attend_copy,
        mixing_terms[0],
        mixing_terms[1],
        mixing_weight,
        mixing_copy,
        expand_terms[0],
        expand_terms[1],
        expand_weight,
        expand_copy,
        shrink_terms[0],
        shrink_terms[1],
        shrink_weight,
        shrink_copy,
        vector_moment,
        vector_square,
        vector_weight,
        trust_norms,
    )


def solution(mesh):
    return jax.shard_map(
        per_device,
        mesh=mesh,
        in_specs=(
            P("dp", "mp", None),
            P("dp", "mp"),
            P(),
            P("dp", "mp", None),
            P(),
            P(),
            P(),
            P("dp", None, "mp"),
            P("dp", None, "mp"),
            P("dp", None, "mp"),
            P("dp", "mp"),
            P("dp", "mp"),
            P("dp", "mp"),
            P("dp", "mp"),
            P("dp", "mp"),
            P("dp", "mp"),
            P("dp", "mp"),
            P("dp", "mp"),
            P("dp", "mp"),
        ),
        out_specs=(
            P("dp", "mp", None),
            P("dp", "mp", None),
            P(),
            P(),
            P("dp", None, "mp"),
            P("dp", None, "mp"),
            P("dp", None, "mp"),
            P("dp", None, "mp"),
            P("dp", "mp"),
            P("dp", "mp"),
            P("dp", "mp"),
            P("dp", "mp"),
            P("dp", "mp"),
            P("dp", "mp"),
            P("dp", "mp"),
            P("dp", "mp"),
            P("dp", "mp"),
            P("dp", "mp"),
            P("dp", "mp"),
            P("dp", "mp"),
            P(),
            P(),
            P(),
            P(),
        ),
        check_vma=False,
    )
```

profile of v0, /device:TPU:0, one launch (start us, length us, event | category | flops | bytes accessed | tf_op | source)
XLA Modules:
  0.0 1049.7 jit_solution(7092816687073616570)
XLA Ops:
  17.4 27.1 %all_gather.26 = bf16[768,384]{1,0:T(8,128)(2,1)} all-gather(bf16[48,384]{1,0:T(8,128)(2,1)S(1)} %convert_element_type.190), channel_id=1, replica_groups=mesh['dp'=16,'mp'=2] {'dp'}, dimensions={0}, use_global_device_ids=true | all-gather | bytes 626688 | tf_op jit(solution)/shard_map/all_gather | solution.py:138
  57.2 35.0 %all-gather.8.cloned.1.call-done = bf16[1,1568,768]{2,1,0:T(8,128)(2,1)} async-done(((bf16[1,784,768]{2,1,0:T(8,128)(2,1)}), bf16[1,1568,768]{2,1,0:T(8,128)(2,1)}) %all-gather.8.cloned.1.call-update) | async-done | bytes 2408464 | tf_op jit(solution)/shard_map/all_gather | solution.py:153
  119.4 113.2 %while.54 = (s32[]{:T(128)}, bf16[6,1568,64]{2,1,0:T(8,128)(2,1)}, f32[6,1568]{1,0:T(8,128)}, bf16[6,1568,64]{2,1,0:T(8,128)(2,1)S(1)}, bf16[6,1568,64]{2,1,0:T(...) while((s32[]{:T(128)}, bf16[6,1568,64]{2,1,0:T(8,128)(2,1)}, ...), condition=%wide.region_7.8_spmd, body=%wide.region_2.7_spmd.sunk | while | flops 325766912 | bytes 37697460 | solution.py:161
  121.4 14.3 %while.57 = (s32[]{:T(128)}, bf16[2,784,64]{1,2,0:T(8,128)(2,1)S(1)}, f32[2,784]{1,0:T(2,128)S(1)}, bf16[2,784,64]{2,1,0:T(8,128)(2,1)S(1)}, bf16[1568,64]{1,0:T...) while((s32[]{:T(128)}, bf16[2,784,64]{1,2,0:T(8,128)(2,1)S(1)}, ...), condition=%wide.region_6.6_spmd, body=%wide.region_3.5_spmd.sunk | while | flops 325766912 | bytes 35463932 | solution.py:47
  159.2 14.3 %while.57 = (s32[]{:T(128)}, bf16[2,784,64]{1,2,0:T(8,128)(2,1)S(1)}, f32[2,784]{1,0:T(2,128)S(1)}, bf16[2,784,64]{2,1,0:T(8,128)(2,1)S(1)}, bf16[1568,64]{1,0:T...) while((s32[]{:T(128)}, bf16[2,784,64]{1,2,0:T(8,128)(2,1)S(1)}, ...), condition=%wide.region_6.6_spmd, body=%wide.region_3.5_spmd.sunk | while | flops 325766912 | bytes 35463932 | solution.py:47
  196.9 14.3 %while.57 = (s32[]{:T(128)}, bf16[2,784,64]{1,2,0:T(8,128)(2,1)S(1)}, f32[2,784]{1,0:T(2,128)S(1)}, bf16[2,784,64]{2,1,0:T(8,128)(2,1)S(1)}, bf16[1568,64]{1,0:T...) while((s32[]{:T(128)}, bf16[2,784,64]{1,2,0:T(8,128)(2,1)S(1)}, ...), condition=%wide.region_6.6_spmd, body=%wide.region_3.5_spmd.sunk | while | flops 325766912 | bytes 35463932 | solution.py:47
  243.5 33.3 %reduce-scatter.9.cloned.1.call-done = bf16[1,784,768]{2,1,0:T(8,128)(2,1)} async-done(((bf16[1,1568,768]{2,1,0:T(8,128)(2,1)}), bf16[1,784,768]{2,1,0:T(8,128)(2,1)}) %reduce-scatter.9.cloned.1.call-update) | async-done | bytes 1204240 | tf_op jit(solution)/shard_map/reduce_scatter | solution.py:167
  283.4 38.6 %all-gather.14.cloned.1.call-done = bf16[768,1536]{1,0:T(8,128)(2,1)} async-done(((bf16[48,1536]{1,0:T(8,128)(2,1)}), bf16[768,1536]{1,0:T(8,128)(2,1)}) %all-gather.14.cloned.1.call-update) | async-done | bytes 2359312 | tf_op jit(solution)/shard_map/all_gather | solution.py:139
  322.0 37.5 %all-gather.12.cloned.1.call-done = bf16[1,1568,768]{2,1,0:T(8,128)(2,1)} async-done(((bf16[1,784,768]{2,1,0:T(8,128)(2,1)}), bf16[1,1568,768]{2,1,0:T(8,128)(2,1)}) %all-gather.12.cloned.1.call-update) | async-done | bytes 2408464 | tf_op jit(solution)/shard_map/all_gather | solution.py:174
  359.5 27.4 %multiply_convert_fusion.1 = (bf16[1568,1536]{1,0:T(8,128)(2,1)}, f32[1568,1536]{1,0:T(8,128)}, f32[1568,1536]{1,0:T(8,128)}) fusion(f32[1536]{0:T(1024)S(1)} %dynamic_slice.51, bf16[768,1536]{1,0:T(8,128)(2,1)} %all-gather.14.cloned.1.call-done, bf16[1,1568,768]{2,1,0:T(8,128)(2,1)} %all-gather.12.cloned.1.call-done), kind=kOutput, calls=%fused_computation.54 | convolution fusion | flops 3858333696 | bytes 28858368 | tf_op jit(solution)/shard_map/dot_general | solution.py:175
  407.5 75.7 %reduce-scatter.23.cloned.1.call-done = f32[48,1536]{1,0:T(8,128)} async-done(((f32[768,1536]{1,0:T(8,128)}), f32[48,1536]{1,0:T(8,128)}) %reduce-scatter.23.cloned.1.call-update) | async-done | bytes 294928 | tf_op jit(solution)/shard_map/reduce_scatter | solution.py:231
  486.0 41.3 %all-gather.16.cloned.1.call-done = bf16[768,1536]{1,0:T(8,128)(2,1)} async-done(((bf16[48,1536]{1,0:T(8,128)(2,1)}), bf16[768,1536]{1,0:T(8,128)(2,1)}) %all-gather.16.cloned.1.call-update) | async-done | bytes 2359312 | tf_op jit(solution)/shard_map/all_gather | solution.py:140
  557.2 25.5 %reduce-scatter.13.cloned.1.call-done = bf16[1,784,768]{2,1,0:T(8,128)(2,1)} async-done(((bf16[1,1568,768]{2,1,0:T(8,128)(2,1)}), bf16[1,784,768]{2,1,0:T(8,128)(2,1)}) %reduce-scatter.13.cloned.1.call-update) | async-done | bytes 1204240 | tf_op jit(solution)/shard_map/reduce_scatter | solution.py:200
  586.0 34.1 %reduce-scatter.11.cloned.1.call-done = bf16[1,784,768]{2,1,0:T(8,128)(2,1)} async-done(((bf16[1,1568,768]{2,1,0:T(8,128)(2,1)}), bf16[1,784,768]{2,1,0:T(8,128)(2,1)}) %reduce-scatter.11.cloned.1.call-update) | async-done | bytes 1204240 | tf_op jit(solution)/shard_map/reduce_scatter | solution.py:181
  636.1 27.2 %all-gather.20.cloned.1.call-done = bf16[1,1568,768]{2,1,0:T(8,128)(2,1)} async-done(((bf16[1,784,768]{2,1,0:T(8,128)(2,1)}), bf16[1,1568,768]{2,1,0:T(8,128)(2,1)}) %all-gather.20.cloned.1.call-update) | async-done | bytes 2408464 | tf_op jit(solution)/shard_map/all_gather | solution.py:207
  674.8 196.0 %while.56 = (s32[]{:T(128)}, bf16[6,1568,64]{2,1,0:T(8,128)(2,1)}, bf16[6,1568,64]{1,2,0:T(8,128)(2,1)}, bf16[6,1568,64]{1,2,0:T(8,128)(2,1)}, bf16[6,1568,64]{2...) while((s32[]{:T(128)}, bf16[6,1568,64]{2,1,0:T(8,128)(2,1)}, ...), condition=%wide.region_19.20_spmd, body=%wide.region_15.19_spmd.sunk | while | flops 797145344 | bytes 91663784 | solution.py:215
  680.1 23.6 %while.58 = (s32[]{:T(128)}, f32[1568,64]{0,1:T(8,128)S(1)}, f32[1568,64]{0,1:T(8,128)}, bf16[2,784,64]{1,2,0:T(8,128)(2,1)}, bf16[2,784,64]{2,1,0:T(8,128)(2,1)...) while((s32[]{:T(128)}, f32[1568,64]{0,1:T(8,128)S(1)}, ...), condition=%wide.region_18.18_spmd.clone, body=%wide.region_16.17_spmd.clone.sunk | while | flops 797145344 | bytes 86947512 | solution.py:81
  712.7 23.6 %while.58 = (s32[]{:T(128)}, f32[1568,64]{0,1:T(8,128)S(1)}, f32[1568,64]{0,1:T(8,128)}, bf16[2,784,64]{1,2,0:T(8,128)(2,1)}, bf16[2,784,64]{2,1,0:T(8,128)(2,1)...) while((s32[]{:T(128)}, f32[1568,64]{0,1:T(8,128)S(1)}, ...), condition=%wide.region_18.18_spmd.clone, body=%wide.region_16.17_spmd.clone.sunk | while | flops 797145344 | bytes 86947512 | solution.py:81
  745.4 23.6 %while.58 = (s32[]{:T(128)}, f32[1568,64]{0,1:T(8,128)S(1)}, f32[1568,64]{0,1:T(8,128)}, bf16[2,784,64]{1,2,0:T(8,128)(2,1)}, bf16[2,784,64]{2,1,0:T(8,128)(2,1)...) while((s32[]{:T(128)}, f32[1568,64]{0,1:T(8,128)S(1)}, ...), condition=%wide.region_18.18_spmd.clone, body=%wide.region_16.17_spmd.clone.sunk | while | flops 797145344 | bytes 86947512 | solution.py:81
  778.1 23.6 %while.58 = (s32[]{:T(128)}, f32[1568,64]{0,1:T(8,128)S(1)}, f32[1568,64]{0,1:T(8,128)}, bf16[2,784,64]{1,2,0:T(8,128)(2,1)}, bf16[2,784,64]{2,1,0:T(8,128)(2,1)...) while((s32[]{:T(128)}, f32[1568,64]{0,1:T(8,128)S(1)}, ...), condition=%wide.region_18.18_spmd.clone, body=%wide.region_16.17_spmd.clone.sunk | while | flops 797145344 | bytes 86947512 | solution.py:81
  810.7 23.6 %while.58 = (s32[]{:T(128)}, f32[1568,64]{0,1:T(8,128)S(1)}, f32[1568,64]{0,1:T(8,128)}, bf16[2,784,64]{1,2,0:T(8,128)(2,1)}, bf16[2,784,64]{2,1,0:T(8,128)(2,1)...) while((s32[]{:T(128)}, f32[1568,64]{0,1:T(8,128)S(1)}, ...), condition=%wide.region_18.18_spmd.clone, body=%wide.region_16.17_spmd.clone.sunk | while | flops 797145344 | bytes 86947512 | solution.py:81
  843.4 23.6 %while.58 = (s32[]{:T(128)}, f32[1568,64]{0,1:T(8,128)S(1)}, f32[1568,64]{0,1:T(8,128)}, bf16[2,784,64]{1,2,0:T(8,128)(2,1)}, bf16[2,784,64]{2,1,0:T(8,128)(2,1)...) while((s32[]{:T(128)}, f32[1568,64]{0,1:T(8,128)S(1)}, ...), condition=%wide.region_18.18_spmd.clone, body=%wide.region_16.17_spmd.clone.sunk | while | flops 797145344 | bytes 86947512 | solution.py:81
  927.8 59.8 %reduce-scatter.17.cloned.1.call-done = f32[48,3,384]{2,0,1:T(8,128)} async-done(((f32[768,3,384]{2,0,1:T(8,128)}), f32[48,3,384]{2,0,1:T(8,128)}) %reduce-scatter.17.cloned.1.call-update) | async-done | bytes 221200 | tf_op jit(solution)/shard_map/reduce_scatter | solution.py:228
  990.8 40.3 %all-reduce = (f32[768]{0:T(1024)}, f32[12,768]{1,0:T(8,128)S(1)}, f32[4,2]{1,0:T(4,128)S(1)}) all-reduce(f32[768]{0:T(1024)S(1)} %get-tuple-element.440, f32[12,768]{1,0:T(8,128)S(1)} %concatenate.7, f32[4,2]{1,0:T(4,128)S(1)} %pad_maximum_fusion.1), channel_id=1, replica_groups=mesh['dp'=16,'mp'=2] {'dp','mp'}, use_global_device_ids=true, to_apply=%region_24.25 | all-reduce | flops 9992 | bytes 79936 | tf_op jit(solution)/shard_map/psum | solution.py:279
  (831 shorter events, 566.8 us)
Async XLA Ops:
  7.2 47.3 %all-gather.10.cloned.1.call-start = ((), (), s32[]{:S(2)}) async-start(), calls=%async_computation.9 | async-start | bytes 1880064 | tf_op jit(solution)/shard_map/all_gather | solution.py:137
  9.0 83.3 %all-gather.8.cloned.1.call-start = ((), (), s32[]{:S(2)}) async-start(), calls=%async_computation.8 | async-start | bytes 3612672 | tf_op jit(solution)/shard_map/all_gather | solution.py:153
  17.3 259.5 %reduce-scatter.9.cloned.1.call-start = ((), (), s32[]{:S(2)}) async-start(), calls=%async_computation.10 | async-start | bytes 3612672 | tf_op jit(solution)/shard_map/reduce_scatter | solution.py:167
  241.4 80.6 %all-gather.14.cloned.1.call-start = ((), (), s32[]{:S(2)}) async-start(), calls=%async_computation.12 | async-start | bytes 2506752 | tf_op jit(solution)/shard_map/all_gather | solution.py:139
  243.0 116.5 %all-gather.12.cloned.1.call-start = ((), (), s32[]{:S(2)}) async-start(), calls=%async_computation.11 | async-start | bytes 3612672 | tf_op jit(solution)/shard_map/all_gather | solution.py:174
  281.9 115.7 %all-gather.18.cloned.1.call-start = ((), (), s32[]{:S(2)}) async-start(), calls=%async_computation.15 | async-start | bytes 3612672 | tf_op jit(solution)/shard_map/all_gather | solution.py:188
  282.5 200.7 %reduce-scatter.23.cloned.1.call-start = ((), (), s32[]{:S(2)}) async-start(), calls=%async_computation.22 | async-start | bytes 5013504 | tf_op jit(solution)/shard_map/reduce_scatter | solution.py:231
  407.5 119.9 %all-gather.16.cloned.1.call-start = ((), (), s32[]{:S(2)}) async-start(), calls=%async_computation.13 | async-start | bytes 2506752 | tf_op jit(solution)/shard_map/all_gather | solution.py:140
  485.8 96.8 %reduce-scatter.13.cloned.1.call-start = ((), (), s32[]{:S(2)}) async-start(), calls=%async_computation.16 | async-start | bytes 3612672 | tf_op jit(solution)/shard_map/reduce_scatter | solution.py:200
  548.5 71.7 %reduce-scatter.11.cloned.1.call-start = ((), (), s32[]{:S(2)}) async-start(), calls=%async_computation.14 | async-start | bytes 3612672 | tf_op jit(solution)/shard_map/reduce_scatter | solution.py:181
  557.1 106.2 %all-gather.20.cloned.1.call-start = ((), (), s32[]{:S(2)}) async-start(), calls=%async_computation.17 | async-start | bytes 3612672 | tf_op jit(solution)/shard_map/all_gather | solution.py:207
  626.5 265.9 %reduce-scatter.21.cloned.1.call-start = ((), (), s32[]{:S(2)}) async-start(), calls=%async_computation.21 | async-start | bytes 5013504 | tf_op jit(solution)/shard_map/reduce_scatter | solution.py:230
  636.0 264.2 %reduce-scatter.19.cloned.1.call-start = ((), (), s32[]{:S(2)}) async-start(), calls=%async_computation.20 | async-start | bytes 1253376 | tf_op jit(solution)/shard_map/reduce_scatter | solution.py:229
  673.0 243.0 %reduce-scatter.15.cloned.1.call-start = ((), (), s32[]{:S(2)}) async-start(), calls=%async_computation.18 | async-start | bytes 3612672 | tf_op jit(solution)/shard_map/reduce_scatter | solution.py:236
  880.5 107.2 %reduce-scatter.17.cloned.1.call-start = ((), (), s32[]{:S(2)}) async-start(), calls=%async_computation.19 | async-start | bytes 3760128 | tf_op jit(solution)/shard_map/reduce_scatter | solution.py:228
  894.3 145.9 %copy-start.31 = (f32[48,1536]{1,0:T(8,128)}, f32[48,1536]{1,0:T(8,128)S(1)}, u32[]{:S(2)}) copy-start(f32[48,1536]{1,0:T(8,128)S(1)} %get-tuple-element.434) | copy-start | bytes 884740
  894.3 145.9 %copy-start.32 = (f32[48,1536]{1,0:T(8,128)}, f32[48,1536]{1,0:T(8,128)S(1)}, u32[]{:S(2)}) copy-start(f32[48,1536]{1,0:T(8,128)S(1)} %get-tuple-element.435) | copy-start | bytes 884740
  901.8 139.3 %copy-start.46 = (f32[48,384]{1,0:T(8,128)}, f32[48,384]{1,0:T(8,128)S(1)}, u32[]{:S(2)}) copy-start(f32[48,384]{1,0:T(8,128)S(1)} %get-tuple-element.432) | copy-start | bytes 221188
  901.8 139.3 %copy-start.47 = (f32[48,384]{1,0:T(8,128)}, f32[48,384]{1,0:T(8,128)S(1)}, u32[]{:S(2)}) copy-start(f32[48,384]{1,0:T(8,128)S(1)} %get-tuple-element.433) | copy-start | bytes 221188
  923.9 114.2 %copy-start.43 = (f32[12,768]{1,0:T(8,128)S(1)}, f32[12,768]{1,0:T(8,128)}, u32[]{:S(2)}) copy-start(f32[12,768]{1,0:T(8,128)} %param.31) | copy-start | bytes 110596
  923.9 114.2 %copy-start.66 = (f32[12,768]{1,0:T(8,128)S(1)}, f32[12,768]{1,0:T(8,128)}, u32[]{:S(2)}) copy-start(f32[12,768]{1,0:T(8,128)} %param.33) | copy-start | bytes 110596
  924.0 115.3 %copy-start.28 = (f32[48,1536]{1,0:T(8,128)S(1)}, f32[48,1536]{1,0:T(8,128)}, u32[]{:S(2)}) copy-start(f32[48,1536]{1,0:T(8,128)} %param.43) | copy-start | bytes 884740
  924.0 115.3 %copy-start.29 = (f32[48,1536]{1,0:T(8,128)S(1)}, f32[48,1536]{1,0:T(8,128)}, u32[]{:S(2)}) copy-start(f32[48,1536]{1,0:T(8,128)} %get-tuple-element.436) | copy-start | bytes 884740
  924.0 115.3 %copy-start.30 = (f32[48,1536]{1,0:T(8,128)S(1)}, f32[48,1536]{1,0:T(8,128)}, u32[]{:S(2)}) copy-start(f32[48,1536]{1,0:T(8,128)} %get-tuple-element.437) | copy-start | bytes 884740
  (198 other events, 1717.0 us)
Sparse Core Ops, SparseCore 0:
  11.0 43.5 all-gather.9
  56.7 35.5 all-gather.7
  241.5 35.2 reduce-scatter.8
  279.8 42.2 all-gather.13
  324.1 35.3 all-gather.11
  361.0 36.6 all-gather.17
  407.6 75.5 reduce-scatter.22
  486.0 41.2 all-gather.15
  548.6 34.0 reduce-scatter.12
  584.8 35.2 reduce-scatter.10
  626.6 36.6 all-gather.19
  667.0 75.5 reduce-scatter.20
  747.2 57.1 reduce-scatter.18
  880.6 35.2 reduce-scatter.14
  919.7 67.9 reduce-scatter.16
where the time goes:
time: 1060 us; the launch traced here: 1050 us
  waiting for transfers between devices  442 us (42%)
  matrix products  252 us (24%)
  local copies, waits for them, and re-layouts  182 us (17%)
  other arithmetic  81.4 us (8%)
  blocking collectives  67.4 us (6%)
  between operations  20.5 us (2%)
    reduce_scatter x1, waiting for transfers between devices, per_device(): lax.psum_scatter(shrink_grad, 'dp', scatter_dimension=0, tiled=True)  75.7 us
    reduce_scatter x1, waiting for transfers between devices, per_device(): lax.psum_scatter(attend_grad, 'dp', scatter_dimension=0, tiled=True)  59.8 us
    while x264, local copies, waits for them, and re-layouts  51.7 us
    dot_general x12, matrix products, one_block(): result = jnp.dot(attention, values, preferred_element_type=jnp.float32)  46.1 us
    all_gather x1, waiting for transfers between devices, per_device(): lax.all_gather(shrink_master.astype(jnp.bfloat16), 'dp', axis=0, tiled=True)  41.3 us
    psum x1, blocking collectives, per_device(): lax.psum((vector_part, token_part, squares), ('dp', 'mp'))  40.3 us
    all_gather x1, waiting for transfers between devices, per_device(): lax.all_gather(expand_master.astype(jnp.bfloat16), 'dp', axis=0, tiled=True)  38.6 us
    all_gather x1, waiting for transfers between devices, per_device(): lax.all_gather(normed_two, 'mp', axis=1, tiled=True)  37.5 us
  transfers between devices with their start and end apart: 15, of which 13 were waited for; matrix products, arithmetic and copies ran while one was open for 26% of the time, Pallas kernels for 0%

commit v1 on v0

v1 whole, which is shorter than its diff:
```python
import functools

import jax
import jax.numpy as jnp
from jax import lax
from jax.experimental import pallas as pl
from jax.experimental.pallas import tpu as pltpu
from jax.sharding import PartitionSpec as P

HD = 64
PAIR = 2 * HD
STEP = 5
BF = jnp.bfloat16
F32 = jnp.float32
NN = (((1,), (0,)), ((), ()))
NT = (((1,), (1,)), ((), ()))
TN = (((0,), (0,)), ((), ()))
LOG2E = 1.4426950408889634
MESH = pl.DeviceIdType.MESH
VMEM_LIMIT = 60 * 2**20


def dot(a, b, dims=NN):
    return lax.dot_general(a, b, dims, preferred_element_type=F32)


def params(**kw):
    return pltpu.CompilerParams(vmem_limit_bytes=VMEM_LIMIT, **kw)


def anywhere():
    return pl.BlockSpec(memory_space=pl.ANY)


def in_vmem():
    return pl.BlockSpec(memory_space=pltpu.VMEM)


def place():
    dp, x = lax.axis_index("dp"), lax.axis_index("mp")
    return x, dp // 4, lax.rem(dp // 2, 2), lax.rem(dp, 2)


def device(x, z, y, c):
    return ((z * 2 + y) * 2 + c, x)


def neighbours():
    x, z, y, c = place()
    lines = [device(x, lax.rem(z + k, 4), y, c) for k in (1, 2, 3)]
    return lines, device(1 - x, z, y, c), device(x, z, 1 - y, c), device(x, z, y, 1 - c)


def greet():
    lines, over_x, over_y, sibling = neighbours()
    barrier = pltpu.get_barrier_semaphore()
    for other in (*lines, over_x, over_y, sibling):
        pl.semaphore_signal(barrier, inc=1, device_id=other, device_id_type=MESH)
    pl.semaphore_wait(barrier, 6)


def gather_kernel(count, *refs):
    shards, wholes = refs[:count], refs[count : 2 * count]
    own_sem, send_sem, recv_sem = refs[2 * count :]
    x, z, y, c = place()
    lines, over_x, over_y, sibling = neighbours()
    greet()

    def remote(i, slot, src, dst, other):
        return pltpu.make_async_remote_copy(
            src_ref=src,
            dst_ref=dst,
            send_sem=send_sem.at[i, slot],
            recv_sem=recv_sem.at[i, slot],
            device_id=other,
            device_id_type=MESH,
        )

    def own(i):
        return pltpu.make_async_copy(shards[i], wholes[i].at[x, z, y, c], own_sem.at[i])

    def line(i, k):
        return remote(i, k - 1, shards[i], wholes[i].at[x, z, y, c], lines[k - 1])

    def plane(i, slot, other, part):
        view = wholes[i].at[part]
        return remote(i, slot, view, view, other)

    def lane(i, k):
        return (x, slice(None), y, c)

    def step_two(i):
        part = (x, slice(None), y, c)
        return [plane(i, 3, over_x, part), plane(i, 4, over_y, part), plane(i, 7, sibling, part)]

    def step_three(i):
        return [
            plane(i, 5, over_x, (x, pl.ds(0, 2), 1 - y, c)),
            plane(i, 6, over_y, (1 - x, pl.ds(2, 2), y, c)),
            plane(i, 8, sibling, (1 - x, slice(None), y, c)),
            plane(i, 9, sibling, (x, slice(None), 1 - y, c)),
        ]

    def step_four(i):
        return [plane(i, 10, sibling, (1 - x, slice(None), 1 - y, c))]

    started = []

    def start(copies):
        for copy in copies:
            copy.start()
            started.append(copy)

    for i in range(count):
        own(i).start()
        start([line(i, k) for k in (1, 2, 3)])
    for turn in range(count + 2):
        if turn < count:
            i = turn
            own(i).wait()
            for k in (1, 2, 3):
                line(i, k).wait_recv()
            start(step_two(i))
        if 0 <= turn - 1 < count:
            i = turn - 1
            two = step_two(i)
            two[0].wait_recv()
            two[1].wait_recv()
            start(step_three(i))
        if 0 <= turn - 2 < count:
            i = turn - 2
            three = step_three(i)
            three[0].wait_recv()
            three[1].wait_recv()
            start(step_four(i))
    for i in range(count):
        step_two(i)[2].wait_recv()
        step_three(i)[2].wait_recv()
        step_three(i)[3].wait_recv()
        step_four(i)[0].wait_recv()
    for copy in started:
        copy.wait_send()


def gather_all(shards):
    count = len(shards)
    outs = [jax.ShapeDtypeStruct((2, 4, 2, 2, *s.shape), s.dtype) for s in shards]
    wholes = pl.pallas_call(
        functools.partial(gather_kernel, count),
        out_shape=outs,
        in_specs=[anywhere()] * count,
        out_specs=[anywhere()] * count,
        scratch_shapes=[
            pltpu.SemaphoreType.DMA((count,)),
            pltpu.SemaphoreType.DMA((count, 11)),
            pltpu.SemaphoreType.DMA((count, 11)),
        ],
        compiler_params=params(collective_id=0, has_side_effects=True),
        name="gather_weights",
    )(*shards)
    return [w.reshape(2, -1, s.shape[-1]) for w, s in zip(wholes, shards)]


def scatter_kernel(count, *refs):
    grads, totals = refs[:count], refs[count : 2 * count]
    refs = refs[2 * count :]
    mine, sib, diag, side, far = (refs[k * count : (k + 1) * count] for k in range(5))
    own_sem, send_sem, recv_sem = refs[5 * count :]
    x, z, y, c = place()
    lines, over_x, over_y, sibling = neighbours()
    greet()

    def remote(i, slot, src, dst, other):
        return pltpu.make_async_remote_copy(
            src_ref=src,
            dst_ref=dst,
            send_sem=send_sem.at[i, slot],
            recv_sem=recv_sem.at[i, slot],
            device_id=other,
            device_id_type=MESH,
        )

    def add(dst, one, other):
        dst[...] = (one[...].astype(F32) + other[...].astype(F32)).astype(BF)

    def own(i):
        return pltpu.make_async_copy(grads[i].at[:, :, :, c], mine[i], own_sem.at[i])

    def step_one(i):
        return remote(i, 0, grads[i].at[:, :, :, 1 - c], sib[i], sibling)

    def step_two(i):
        return [
            remote(i, 1, mine[i].at[1 - x, pl.ds(0, 2), 1 - y], diag[i].at[0], over_x),
            remote(i, 2, mine[i].at[1 - x, pl.ds(2, 2), 1 - y], diag[i].at[1], over_y),
        ]

    def step_three(i):
        return [
            remote(i, 3, mine[i].at[1 - x, :, y], side[i].at[0], over_x),
            remote(i, 4, mine[i].at[x, :, 1 - y], side[i].at[1], over_y),
        ]

    def step_four(i):
        return [
            remote(i, 4 + k, mine[i].at[x, lax.rem(z + k, 4), y], far[i].at[k - 1], lines[k - 1])
            for k in (1, 2, 3)
        ]

    started = []

    def start(copies):
        for copy in copies:
            copy.start()
            started.append(copy)

    for i in range(count):
        own(i).start()
        start([step_one(i)])
    for turn in range(count + 3):
        if turn < count:
            i = turn
            own(i).wait()
            step_one(i).wait_recv()

            def sweep(n, _, i=i):
                part = (n // 8, lax.rem(n // 2, 4), lax.rem(n, 2))
                add(mine[i].at[part], mine[i].at[part], sib[i].at[part])
                return 0

            lax.fori_loop(0, 16, sweep, 0)
            start(step_two(i))
        if 0 <= turn - 1 < count:
            i = turn - 1
            two = step_two(i)
            for copy in two:
                copy.wait()

            def sweep(n, _, i=i):
                low, high = (x, n, 1 - y), (1 - x, 2 + n, y)
                add(mine[i].at[low], mine[i].at[low], diag[i].at[0, n])
                add(mine[i].at[high], mine[i].at[high], diag[i].at[1, n])
                return 0

            lax.fori_loop(0, 2, sweep, 0)
            start(step_three(i))
        if 0 <= turn - 2 < count:
            i = turn - 2
            three = step_three(i)
            for copy in three:
                copy.wait()

            def sweep(n, _, i=i):
                part = mine[i].at[x, n, y]
                both = side[i][0, n].astype(F32) + side[i][1, n].astype(F32)
                part[...] = (part[...].astype(F32) + both).astype(BF)
                return 0

            lax.fori_loop(0, 4, sweep, 0)
            start(step_four(i))
        if 0 <= turn - 3 < count:
            i = turn - 3
            for copy in step_four(i):
                copy.wait()
            total = mine[i][x, z, y].astype(F32)
            for k in range(3):
                total = total + far[i][k].astype(F32)
            totals[i][...] = total
    for i in range(count):
        step_one(i).wait_send()


def scatter_all(grads, rows):
    count = len(grads)
    widths = [g.shape[-1] for g in grads]
    grads = [g.reshape(2, 4, 2, 2, rows, w) for g, w in zip(grads, widths)]
    return pl.pallas_call(
        functools.partial(scatter_kernel, count),
        out_shape=[jax.ShapeDtypeStruct((rows, w), F32) for w in widths],
        in_specs=[anywhere()] * count,
        out_specs=[in_vmem()] * count,
        scratch_shapes=[pltpu.VMEM((2, 4, 2, rows, w), BF) for w in widths]
        + [pltpu.VMEM((2, 4, 2, rows, w), BF) for w in widths]
        + [pltpu.VMEM((2, 2, rows, w), BF) for w in widths]
        + [pltpu.VMEM((2, 4, rows, w), BF) for w in widths]
        + [pltpu.VMEM((3, rows, w), BF) for w in widths]
        + [
            pltpu.SemaphoreType.DMA((count,)),
            pltpu.SemaphoreType.DMA((count, 8)),
            pltpu.SemaphoreType.DMA((count, 8)),
        ],
        compiler_params=params(collective_id=1, has_side_effects=True),
        name="scatter_grads",
    )(*grads)


def project_kernel(mine_ref, other_ref, w_ref, bias_ref, q_ref, k_ref, v_ref):
    rows = mine_ref.shape[0]
    half = w_ref.shape[2] // 3
    for h in range(2):
        cols = slice(h * half, (h + 1) * half)
        queries = dot(mine_ref[...], w_ref[h, :, :half]) + bias_ref[0:1, cols]
        q_ref[:, cols] = (queries.astype(BF).astype(F32) * HD**-0.5).astype(BF)
        for part, ref in ((0, mine_ref), (1, other_ref)):
            span = slice(part * rows, (part + 1) * rows)
            k_ref[span, cols] = dot(ref[...], w_ref[h, :, half : 2 * half]).astype(BF)
            v_ref[span, cols] = (dot(ref[...], w_ref[h, :, 2 * half :]) + bias_ref[1:2, cols]).astype(BF)


def project(mine, other, weight, bias):
    rows, width = mine.shape
    keys = jax.ShapeDtypeStruct((2 * rows, width), BF)
    return pl.pallas_call(
        project_kernel,
        out_shape=[jax.ShapeDtypeStruct((rows, width), BF), keys, keys],
        in_specs=[in_vmem()] * 4,
        out_specs=[in_vmem()] * 3,
        compiler_params=params(),
        name="project",
    )(mine, other, weight, bias)


def half_lanes():
    lane = lax.broadcasted_iota(jnp.int32, (1, PAIR), 1)
    return lane < HD, lane >= HD


def attend_kernel(q_ref, k_ref, v_ref, o_ref, low_ref, p_ref):
    sides = half_lanes()
    q, k, v = q_ref[...], k_ref[...], v_ref[...]
    outs = []
    for h in range(2):
        s = dot(jnp.where(sides[h], q, jnp.zeros_like(q)), k, NT)
        top = jnp.max(s, axis=-1, keepdims=True)
        e = jnp.exp2(s * LOG2E - top * LOG2E)
        total = jnp.sum(e, axis=-1, keepdims=True)
        p = (e * (1.0 / total)).astype(BF)
        p_ref[h] = p
        outs.append(dot(p, v))
    o = jnp.where(sides[0], outs[0], outs[1])
    o_ref[...] = o
    low_ref[...] = o.astype(BF)


def attend(q, k, v):
    rows, width = q.shape
    keys = k.shape[0]
    pairs = width // PAIR
    of_q = pl.BlockSpec((rows, PAIR), lambda i: (0, i))
    of_k = pl.BlockSpec((keys, PAIR), lambda i: (0, i))
    return pl.pallas_call(
        attend_kernel,
        grid=(pairs,),
        in_specs=[of_q, of_k, of_k],
        out_specs=[of_q, of_q, pl.BlockSpec((2, rows, keys), lambda i: (i, 0, 0))],
        out_shape=[
            jax.ShapeDtypeStruct((rows, width), F32),
            jax.ShapeDtypeStruct((rows, width), BF),
            jax.ShapeDtypeStruct((2 * pairs, rows, keys), BF),
        ],
        compiler_params=params(),
        name="attend",
    )(q, k, v)


def attend_back_kernel(q_ref, k_ref, v_ref, do_ref, o_ref, p_ref, dq_ref, dk_ref, dv_ref):
    sides = half_lanes()
    q, k, v, do = q_ref[...], k_ref[...], v_ref[...], do_ref[...]
    prod = do.astype(F32) * o_ref[...]
    outs, grad_k, grad_v = [], None, None
    for h in range(2):
        do_h = jnp.where(sides[h], do, jnp.zeros_like(do))
        q_h = jnp.where(sides[h], q, jnp.zeros_like(q))
        grad_p = dot(do_h, v, NT)
        row_dot = jnp.sum(jnp.where(sides[h], prod, 0.0), axis=-1, keepdims=True)
        p = p_ref[h]
        ds = (p.astype(F32) * (grad_p - row_dot)).astype(BF)
        outs.append(dot(ds, k))
        more_k, more_v = dot(ds, q_h, TN), dot(p, do_h, TN)
        grad_k = more_k if grad_k is None else grad_k + more_k
        grad_v = more_v if grad_v is None else grad_v + more_v
    dq_ref[...] = (jnp.where(sides[0], outs[0], outs[1]) * HD**-0.5).astype(BF)
    dk_ref[...] = grad_k.astype(BF)
    dv_ref[...] = grad_v.astype(BF)


def attend_back(q, k, v, do, o, p):
    rows, width = q.shape
    keys = k.shape[0]
    pairs = width // PAIR
    of_q = pl.BlockSpec((rows, PAIR), lambda i: (0, i))
    of_k = pl.BlockSpec((keys, PAIR), lambda i: (0, i))
    return pl.pallas_call(
        attend_back_kernel,
        grid=(pairs,),
        in_specs=[of_q, of_k, of_k, of_q, of_q, pl.BlockSpec((2, rows, keys), lambda i: (i, 0, 0))],
        out_specs=[of_q, of_k, of_k],
        out_shape=[
            jax.ShapeDtypeStruct((rows, width), BF),
            jax.ShapeDtypeStruct((keys, width), BF),
            jax.ShapeDtypeStruct((keys, width), BF),
        ],
        compiler_params=params(),
        name="attend_back",
    )(q, k, v, do, o, p)


def normal_parts(h):
    z = jnp.abs(h) * 0.7071067811865476
    t = 1.0 / (1.0 + 0.3275911 * z)
    bell = jnp.exp(-z * z)
    poly = t * (
        0.254829592
        + t * (-0.284496736 + t * (1.421413741 + t * (-1.453152027 + t * 1.061405429)))
    )
    tail = 0.5 * poly * bell
    return jnp.where(h < 0, tail, 1.0 - tail), bell * 0.3989422804014327


def mean_rows(values):
    return jnp.mean(values, axis=-1, keepdims=True)


def middle_kernel(
    x_ref,
    o_ref,
    dy_ref,
    vec_ref,
    bu_ref,
    wm_ref,
    we_ref,
    ws_ref,
    out_ref,
    dx1_ref,
    do_ref,
    gm_ref,
    ge_ref,
    gs_ref,
    gu_ref,
    gv_ref,
    x1_ref,
    a2_ref,
    acc_ref,
    da2_ref,
):
    i = pl.program_id(0)
    half = wm_ref.shape[2]

    @pl.when(i == 0)
    def _():
        x1 = x_ref[...] + vec_ref[4:5]
        for h in range(2):
            x1 = x1 + dot(o_ref[:, h * half : (h + 1) * half], wm_ref[h], NT)
        x1_ref[...] = x1
        centred = x1 - mean_rows(x1)
        scale = lax.rsqrt(mean_rows(centred * centred) + 1e-6)
        a2_ref[...] = (centred * scale * vec_ref[5:6] + vec_ref[6:7]).astype(BF)
        acc_ref[...] = x1 + vec_ref[11:12]
        da2_ref[...] = jnp.zeros_like(da2_ref)

    a2, dy = a2_ref[...], dy_ref[...]
    we, ws = we_ref[0], ws_ref[0]
    hidden = dot(a2, we) + bu_ref[...]
    cdf, density = normal_parts(hidden)
    u = (hidden * cdf).astype(BF)
    du = dot(dy, ws)
    dh = (du * (cdf + hidden * density)).astype(BF)
    acc_ref[...] += dot(u, ws, NT)
    da2_ref[...] += dot(dh, we, NT)
    gs_ref[0] = dot(dy, u, TN).astype(BF)
    ge_ref[0] = dot(a2, dh, TN).astype(BF)
    gu_ref[...] = jnp.sum(dh.astype(F32), axis=0, keepdims=True)

    @pl.when(i == pl.num_programs(0) - 1)
    def _():
        out_ref[...] = acc_ref[...].astype(BF)
        x1 = x1_ref[...]
        top = dy_ref[...].astype(F32)
        centred = x1 - mean_rows(x1)
        scale = lax.rsqrt(mean_rows(centred * centred) + 1e-6)
        xh = centred * scale
        da2 = da2_ref[...]
        e = da2 * vec_ref[5:6]
        dx1 = top + scale * (e - mean_rows(e) - xh * mean_rows(e * xh))
        dx1_ref[...] = dx1
        dxb = dx1.astype(BF)
        for h in range(2):
            cols = slice(h * half, (h + 1) * half)
            do_ref[:, cols] = dot(dxb, wm_ref[h]).astype(BF)
            gm_ref[h] = dot(dxb, o_ref[:, cols], TN).astype(BF)
        gv_ref[0:1] = jnp.sum(dxb.astype(F32), axis=0, keepdims=True)
        gv_ref[1:2] = jnp.sum(da2 * xh, axis=0, keepdims=True)
        gv_ref[2:3] = jnp.sum(da2, axis=0, keepdims=True)
        gv_ref[3:4] = jnp.sum(top, axis=0, keepdims=True)
        gv_ref[4:] = jnp.zeros((4, gv_ref.shape[1]), F32)


def middle(x, o, dy, vectors, wm, we, ws):
    rows, width = x.shape
    hidden = we.shape[2]
    block = 512
    per = hidden // block
    steps = 2 * per
    of_w = pl.BlockSpec((1, width, block), lambda i: (i // per, 0, lax.rem(i, per)))
    of_u = pl.BlockSpec((1, block), lambda i: (0, i))

    def whole(shape):
        return pl.BlockSpec(shape, lambda i: (0,) * len(shape))

    return pl.pallas_call(
        middle_kernel,
        grid=(steps,),
        in_specs=[
            whole((rows, width)),
            whole((rows, width)),
            whole((rows, width)),
            whole(vectors.shape),
            of_u,
            whole(wm.shape),
            of_w,
            of_w,
        ],
        out_specs=[
            whole((rows, width)),
            whole((rows, width)),
            whole((rows, width)),
            whole(wm.shape),
            of_w,
            of_w,
            of_u,
            whole((8, width)),
        ],
        out_shape=[
            jax.ShapeDtypeStruct((rows, width), BF),
            jax.ShapeDtypeStruct((rows, width), F32),
            jax.ShapeDtypeStruct((rows, width), BF),
            jax.ShapeDtypeStruct(wm.shape, BF),
            jax.ShapeDtypeStruct(we.shape, BF),
            jax.ShapeDtypeStruct(ws.shape, BF),
            jax.ShapeDtypeStruct((1, 2 * hidden), F32),
            jax.ShapeDtypeStruct((8, width), F32),
        ],
        scratch_shapes=[
            pltpu.VMEM((rows, width), F32),
            pltpu.VMEM((rows, width), BF),
            pltpu.VMEM((rows, width), F32),
            pltpu.VMEM((rows, width), F32),
        ],
        compiler_params=params(),
        name="middle",
    )(x, o, dy, vectors, vectors[7:11].reshape(1, -1), wm, we, ws)


def unproject_kernel(
    mine_ref, other_ref, dq_ref, dk_ref, dv_ref, w_ref, da_ref, send_ref, gw_ref, gv_ref
):
    rows = mine_ref.shape[0]
    half = w_ref.shape[2] // 3
    da, send = None, None
    gv_ref[...] = jnp.zeros_like(gv_ref)
    for h in range(2):
        cols = slice(h * half, (h + 1) * half)
        dq = dq_ref[:, cols]
        dk, dv = dk_ref[:, cols], dv_ref[:, cols]
        wq, wk, wv = (w_ref[h, :, n * half : (n + 1) * half] for n in range(3))
        mine = dot(dq, wq, NT) + dot(dk[:rows], wk, NT) + dot(dv[:rows], wv, NT)
        other = dot(dk[rows:], wk, NT) + dot(dv[rows:], wv, NT)
        da = mine if da is None else da + mine
        send = other if send is None else send + other
        a, b = mine_ref[...], other_ref[...]
        gw_ref[h, :, :half] = dot(a, dq, TN).astype(BF)
        gw_ref[h, :, half : 2 * half] = (dot(a, dk[:rows], TN) + dot(b, dk[rows:], TN)).astype(BF)
        gw_ref[h, :, 2 * half :] = (dot(a, dv[:rows], TN) + dot(b, dv[rows:], TN)).astype(BF)
        gv_ref[0:1, cols] = jnp.sum(dq.astype(F32), axis=0, keepdims=True)
        gv_ref[1:2, cols] = jnp.sum(dv.astype(F32), axis=0, keepdims=True)
    da_ref[...] = da
    send_ref[...] = send.astype(BF)


def unproject(mine, other, dq, dk, dv, weight):
    rows, width = mine.shape
    return pl.pallas_call(
        unproject_kernel,
        out_shape=[
            jax.ShapeDtypeStruct((rows, width), F32),
            jax.ShapeDtypeStruct((rows, width), BF),
            jax.ShapeDtypeStruct(weight.shape, BF),
            jax.ShapeDtypeStruct((8, width), F32),
        ],
        in_specs=[in_vmem()] * 6,
        out_specs=[in_vmem()] * 4,
        compiler_params=params(),
        name="unproject",
    )(mine, other, dq, dk, dv, weight)


def lamb_terms(weight, moment, square, gradient):
    moment_new = 0.5 * moment + 0.5 * gradient
    square_new = 0.5 * square + 0.5 * gradient * gradient
    correct = 1.0 - 0.5**STEP
    update = moment_new / correct / (jnp.sqrt(square_new / correct) + 1e-06) + 0.01 * weight
    return (
        moment_new,
        square_new,
        update,
        jnp.stack([jnp.sum(weight * weight), jnp.sum(update * update)]),
    )


def lamb_apply(weight, update, norms):
    renewed = weight - 0.5 * norms[0] / (norms[1] + 1e-06) * update
    return (renewed, renewed.astype(BF))


def per_device(
    patches,
    cube_mask,
    mask_token,
    cotangent,
    vectors,
    vector_first,
    vector_second,
    attend_master,
    attend_first,
    attend_second,
    mixing_master,
    mixing_first,
    mixing_second,
    expand_master,
    expand_first,
    expand_second,
    shrink_master,
    shrink_first,
    shrink_second,
):
    clips, rows, width = patches.shape
    axis = lax.axis_size("dp")
    own_rows = attend_master.shape[0]
    direct = axis == 16 and lax.axis_size("mp") == 2
    masters = [
        attend_master.reshape(own_rows, -1),
        mixing_master,
        expand_master,
        shrink_master,
    ]
    shards = [m.astype(BF) for m in masters]
    if direct:
        wa, wm, we, ws = gather_all(shards)
    else:
        wa, wm, we, ws = (
            lax.all_gather(lax.all_gather(s, "dp", axis=0, tiled=True), "mp", axis=0) for s in shards
        )
    swap = [(0, 1), (1, 0)]
    chosen = cube_mask[0, :, None] > 0
    x = jnp.where(chosen, mask_token, patches[0].astype(F32))
    centred = x - mean_rows(x)
    scale = lax.rsqrt(mean_rows(centred * centred) + 1e-6)
    a1 = (centred * scale * vectors[0] + vectors[1]).astype(BF)
    a1_other = lax.ppermute(a1, "mp", swap)
    q, k, v = project(a1, a1_other, wa, vectors[2:4])
    o, o_low, p = attend(q, k, v)
    dy = cotangent[0]
    block_out, dx1, do, gm, ge, gs, gu, gv = middle(x, o_low, dy, vectors, wm, we, ws)
    dq, dk, dv = attend_back(q, k, v, do, o, p)
    da1, da1_send, ga, gqv = unproject(a1, a1_other, dq, dk, dv, wa)
    da1 = da1 + lax.ppermute(da1_send, "mp", swap).astype(F32)
    grads = [ga, gm, ge, gs]
    if direct:
        totals = scatter_all(grads, own_rows)
    else:
        totals = []
        for g in grads:
            g = lax.psum_scatter(g, "mp", scatter_dimension=0, tiled=True)
            totals.append(
                lax.psum_scatter(g[0].astype(F32), "dp", scatter_dimension=0, tiled=True)
            )
    xh = centred * scale
    e = da1 * vectors[0]
    dx = dx1 + scale * (e - mean_rows(e) - xh * mean_rows(e * xh))
    patch_grad = jnp.where(chosen, 0.0, dx).astype(BF)
    token_part = jnp.sum(jnp.where(chosen, dx, 0.0), axis=0)
    vector_part = jnp.concatenate(
        [
            jnp.sum(da1 * xh, axis=0)[None],
            jnp.sum(da1, axis=0)[None],
            gqv[0:2],
            gv[0:3],
            gu.reshape(4, width),
            gv[3:4],
        ],
        axis=0,
    )
    terms = [
        lamb_terms(w, m, s, g)
        for w, m, s, g in zip(
            masters,
            [attend_first.reshape(own_rows, -1), mixing_first, expand_first, shrink_first],
            [attend_second.reshape(own_rows, -1), mixing_second, expand_second, shrink_second],
            totals,
        )
    ]
    squares = jnp.stack([t[3] for t in terms])
    vector_total, token_grad, square_total = lax.psum(
        (vector_part, token_part, squares), ("dp", "mp")
    )
    trust_norms = jnp.sqrt(square_total)
    results = []
    for n, (w, t) in enumerate(zip(masters, terms)):
        group = [t[0], t[1], *lamb_apply(w, t[2], trust_norms[n])]
        if n == 0:
            group = [g.reshape(attend_master.shape) for g in group]
        results.extend(group)
    vector_moment = 0.5 * vector_first + 0.5 * vector_total
    vector_square = 0.5 * vector_second + 0.5 * vector_total * vector_total
    correct = 1.0 - 0.5**STEP
    vector_update = (
        vector_moment / correct / (jnp.sqrt(vector_square / correct) + 1e-06) + 0.01 * vectors
    )
    row_weight = jnp.sqrt(jnp.sum(vectors * vectors, axis=-1, keepdims=True))
    row_update = jnp.sqrt(jnp.sum(vector_update * vector_update, axis=-1, keepdims=True))
    vector_weight = vectors - 0.5 * row_weight / (row_update + 1e-06) * vector_update
    return (
        block_out[None],
        patch_grad[None],
        token_grad,
        vector_total[11],
        *results,
        vector_moment,
        vector_square,
        vector_weight,
        trust_norms,
    )


def solution(mesh):
    rows = P("dp", "mp", None)
    flat = P("dp", "mp")
    deep = P("dp", None, "mp")
    copied = P()
    return jax.shard_map(
        per_device,
        mesh=mesh,
        in_specs=(rows, flat, copied, rows, copied, copied, copied, *[deep] * 3, *[flat] * 9),
        out_specs=(rows, rows, copied, copied, *[deep] * 4, *[flat] * 12, *[copied] * 4),
        check_vma=False,
    )
```

time: 1060 us -> 450 us (0.42)
  waiting for transfers between devices: 442 us -> 0.01 us
  Pallas kernels: 0 us -> 340 us
  matrix products: 252 us -> 0 us
  local copies, waits for them, and re-layouts: 182 us -> 10.6 us
  other arithmetic: 81.4 us -> 38.6 us
  blocking collectives: 67.4 us -> 41.8 us
  between operations: 20.5 us -> 6.78 us
    pallas_call x0 -> x7, Pallas kernels: none -> 340 us  [the longest x1 99.7 us: scatter_all(): pl.pallas_call(functools.partial(scatter_kernel, count), out_shape=[jax.S...]
    dot_general x96 -> x0, matrix products: 252 us -> none  [the longest x12 46.1 us: one_block(): result = jnp.dot(attention, values, preferred_element_type=jnp.float32)]
    reduce_scatter x8 -> x0, waiting for transfers between devices: 241 us -> none  [the longest x1 75.7 us: per_device(): lax.psum_scatter(shrink_grad, 'dp', scatter_dimension=0, tiled=True)]
    all_gather x7 -> x0, waiting for transfers between devices: 200 us -> none  [the longest x1 41.3 us: per_device(): lax.all_gather(shrink_master.astype(jnp.bfloat16), 'dp', axis=0, tiled=True)]
    while x279 -> x0, local copies, waits for them, and re-layouts: 70.6 us -> none
    dynamic_update_slice x39 -> x0, local copies, waits for them, and re-layouts: 30.5 us -> none  [the longest x24 29.2 us: per_device(): lax.map(head_forward, (query_heads, key_heads, value_heads))]
    reduce_sum x24 -> x5, other arithmetic: 38.2 us -> 10.7 us  [the longest x2 3.69 us: mean_rows(): return jnp.mean(values, axis=-1, keepdims=True)]
    all_gather x1 -> x0, blocking collectives: 27.1 us -> none  [per_device(): lax.all_gather(mixing_master.astype(jnp.bfloat16), 'dp', axis=0, tiled=True)]
  transfers between devices with their start and end apart: 15 -> 2, of which waited for: 13 -> 0; matrix products, arithmetic and copies ran while one was open for 26% -> 5% of each run, Pallas kernels for 0% -> 41%
where the time goes in v1:
time: 450 us; the launch traced here: 443 us
  Pallas kernels  340 us (76%)
  blocking collectives  41.8 us (9%)
  other arithmetic  38.6 us (9%)
  local copies, waits for them, and re-layouts  10.6 us (2%)
  between operations  6.78 us (2%)
  starting transfers between devices  4.75 us (1%)
    pallas_call x1, Pallas kernels, scatter_all(): pl.pallas_call(functools.partial(scatter_kernel, count), out_shape=[jax.S...  99.7 us
    pallas_call x1, Pallas kernels, gather_all(): pl.pallas_call(functools.partial(gather_kernel, count), out_shape=outs, i...  80.9 us
    pallas_call x1, Pallas kernels, middle(): pl.pallas_call(middle_kernel, grid=(steps,), in_specs=[whole((rows, width...  45.4 us
    pallas_call x1, Pallas kernels, attend(): pl.pallas_call(attend_kernel, grid=(pairs,), in_specs=[of_q, of_k, of_k],...  42 us
    psum x1, blocking collectives, per_device(): lax.psum((vector_part, token_part, squares), ('dp', 'mp'))  41.8 us
    pallas_call x1, Pallas kernels, attend_back(): pl.pallas_call(attend_back_kernel, grid=(pairs,), in_specs=[of_q, of_k, o...  41.3 us
    pallas_call x1, Pallas kernels, unproject(): pl.pallas_call(unproject_kernel, out_shape=[jax.ShapeDtypeStruct((rows, w...  20.3 us
    pallas_call x1, Pallas kernels, project(): pl.pallas_call(project_kernel, out_shape=[jax.ShapeDtypeStruct((rows, wid...  10.7 us
  transfers between devices with their start and end apart: 2, of which 0 were waited for; matrix products, arithmetic and copies ran while one was open for 5% of the time, Pallas kernels for 41%

profile of v1, /device:TPU:0, one launch (start us, length us, event | category | flops | bytes accessed | tf_op | source)
XLA Modules:
  0.0 442.9 jit_solution(9978082394865585828)
XLA Ops:
  1.5 1.7 fusion
  3.3 2.0 multiply_reduce_fusion.2
  5.4 3.0 add_convert_fusion
  8.4 3.0 collective-permute-start
  16.8 80.9 %gather_weights.1 = (bf16[2,4,2,2,48,1152]{5,4,3,2,1,0:T(8,128)(2,1)}, bf16[2,4,2,2,48,384]{5,4,3,2,1,0:T(8,128)(2,1)}, bf16[2,4,2,2,48,1536]{5,4,3,2,1,0:T(8,128)(2,1)}, bf16[2,4,2,2,48,1536]{5,4,3,2,1,0:T(8,128)(2,1)}) custom-call(bf16[48,1152]{1,0:T(8,128)(2,1)} %convert_element_type.42.refs_0_, bf16[48,384]{1,0:T(8,128)(2,1)} %convert_element_type.43.refs_1_, ...), custom_call_target="tpu_custom_call" | custom-call | tf_op jit(solution)/shard_map/gather_weights/pallas_call | solution.py:148
  97.7 1.6 multiply_reduce_fusion.9
  100.4 10.7 %project.1 = (bf16[784,768]{1,0:T(8,128)(2,1)}, bf16[1568,768]{1,0:T(8,128)(2,1)}, bf16[1568,768]{1,0:T(8,128)(2,1)}) custom-call(bf16[784,768]{1,0:T(8,128)(2,1)} %copy-done.1, bf16[784,768]{1,0:T(8,128)(2,1)} %copy-done.3, bf16[2,768,1152]{2,1,0:T(8,128)(2,1)} %bitcast.68, f32[2,768]{1,0:T(2,128)} %slice.71.bias_ref), custom_call_target="tpu_custom_call" | custom-call | tf_op jit(solution)/shard_map/project/pallas_call | solution.py:313
  111.1 42.0 %attend.1 = (f32[784,768]{1,0:T(8,128)}, bf16[784,768]{1,0:T(8,128)(2,1)}, bf16[12,784,1568]{2,1,0:T(8,128)(2,1)}) custom-call(bf16[784,768]{1,0:T(8,128)(2,1)} %get-tuple-element.54.q_ref, bf16[1568,768]{1,0:T(8,128)(2,1)} %get-tuple-element.55.k_ref, bf16[1568,768]{1,0:T(8,128)(2,1)} %get-tuple-element.56.v_ref), custom_call_target="tpu_custom_call" | custom-call | tf_op jit(solution)/shard_map/attend/pallas_call | solution.py:351
  153.1 45.4 %middle.1 = (bf16[784,768]{1,0:T(8,128)(2,1)}, f32[784,768]{1,0:T(8,128)}, bf16[784,768]{1,0:T(8,128)(2,1)}, bf16[2,768,384]{2,1,0:T(8,128)(2,1)}, bf16[2,768,15...) custom-call(f32[784,768]{1,0:T(8,128)} %get-tuple-element.169.x_ref, ...), custom_call_target="tpu_custom_call" | custom-call | tf_op jit(solution)/shard_map/middle/pallas_call | solution.py:510
  198.5 41.3 %attend_back.1 = (bf16[784,768]{1,0:T(8,128)(2,1)}, bf16[1568,768]{1,0:T(8,128)(2,1)}, bf16[1568,768]{1,0:T(8,128)(2,1)}) custom-call(bf16[784,768]{1,0:T(8,128)(2,1)} %get-tuple-element.54.q_ref, bf16[1568,768]{1,0:T(8,128)(2,1)} %get-tuple-element.55.k_ref, bf16[1568,768]{1,0:T(8,128)(2,1)} %get-tuple-element.56.v_ref, ...), custom_call_target="tpu_custom_call" | custom-call | tf_op jit(solution)/shard_map/attend_back/pallas_call | solution.py:393
  239.8 20.3 %unproject.1 = (f32[784,768]{1,0:T(8,128)}, bf16[784,768]{1,0:T(8,128)(2,1)}, bf16[2,768,1152]{2,1,0:T(8,128)(2,1)}, f32[8,768]{1,0:T(8,128)}) custom-call(bf16[784,768]{1,0:T(8,128)(2,1)} %copy-done.1, bf16[784,768]{1,0:T(8,128)(2,1)} %copy-done.3, bf16[784,768]{1,0:T(8,128)(2,1)} %get-tuple-element.66.dq_ref, bf16[1568,768]{1,0:T(8,128)(2,1)} %get-tuple-element.67.dk_ref, ...), custom_call_target="tpu_custom_call" | custom-call | tf_op jit(solution)/shard_map/unproject/pallas_call | solution.py:582
  260.1 1.7 collective-permute-start.1
  261.9 99.7 %scatter_grads.1 = (f32[48,1152]{1,0:T(8,128)}, f32[48,384]{1,0:T(8,128)}, f32[48,1536]{1,0:T(8,128)}, f32[48,1536]{1,0:T(8,128)}) custom-call(bf16[2,4,2,2,48,1152]{5,4,3,2,1,0:T(8,128)(2,1)} %bitcast.74, bf16[2,4,2,2,48,384]{5,4,3,2,1,0:T(8,128)(2,1)} %bitcast.81, bf16[2,4,2,2,48,1536]{5,4,3,2,1,0:T(8,128)(2,1)} %bitcast.70, ...), custom_call_target="tpu_custom_call" | custom-call | tf_op jit(solution)/shard_map/scatter_grads/pallas_call | solution.py:277
  361.7 3.4 multiply_reduce_fusion.5
  367.6 1.5 maximum_bitcast_fusion.2
  369.1 1.4 maximum_bitcast_fusion.3
  370.5 2.2 multiply_reduce_fusion.11
  372.7 1.9 multiply_reduce_fusion.8
  374.6 2.7 maximum_bitcast_fusion
  378.7 1.7 multiply_reduce_fusion
  381.3 3.4 select_reduce_fusion
  384.8 41.8 %all-reduce = (f32[768]{0:T(1024)}, f32[12,768]{1,0:T(8,128)S(1)}, f32[4,2]{1,0:T(4,128)S(1)}) all-reduce(f32[768]{0:T(1024)S(1)} %get-tuple-element.166, f32[12,768]{1,0:T(8,128)S(1)} %concatenate.3, f32[4,2]{1,0:T(4,128)S(1)} %copy-done.41), channel_id=1, replica_groups=mesh['dp'=16,'mp'=2] {'dp','mp'}, use_global_device_ids=true, to_apply=%region_5.6 | all-reduce | flops 9992 | bytes 79936 | tf_op jit(solution)/shard_map/psum | solution.py:703
  433.1 1.1 fusion.12
  436.1 2.0 fusion.1
  (126 shorter events, 19.7 us)
Async XLA Ops:
  1.5 6.9 %copy-start.37 = (pred[784]{0:T(1024)(128)(4,1)}, pred[784]{0:T(1024)(128)(4,1)S(1)}, u32[]{:S(2)}) copy-start(pred[784]{0:T(1024)(128)(4,1)S(1)} %compare_reduce_fusion) | copy-start | bytes 2356
  5.3 7.4 %copy-start.6 = (f32[48,1536]{1,0:T(8,128)S(1)}, f32[48,1536]{1,0:T(8,128)}, u32[]{:S(2)}) copy-start(f32[48,1536]{1,0:T(8,128)} %param.32) | copy-start | bytes 884740
  5.4 8.1 %copy-start.5 = (f32[48,1536]{1,0:T(8,128)S(1)}, f32[48,1536]{1,0:T(8,128)}, u32[]{:S(2)}) copy-start(f32[48,1536]{1,0:T(8,128)} %param.35) | copy-start | bytes 884740
  5.4 8.7 %copy-start.14 = (f32[48,384]{1,0:T(8,128)S(1)}, f32[48,384]{1,0:T(8,128)}, u32[]{:S(2)}) copy-start(f32[48,384]{1,0:T(8,128)} %param.29) | copy-start | bytes 221188
  5.4 10.0 %copy-start.22 = (f32[48,3,384]{2,0,1:T(8,128)S(1)}, f32[48,3,384]{2,0,1:T(8,128)}, u32[]{:S(2)}) copy-start(f32[48,3,384]{2,0,1:T(8,128)} %param.27) | copy-start | bytes 663556
  8.4 90.9 %copy-start.1 = (bf16[784,768]{1,0:T(8,128)(2,1)}, bf16[784,768]{1,0:T(8,128)(2,1)S(1)}, u32[]{:S(2)}) copy-start(bf16[784,768]{1,0:T(8,128)(2,1)S(1)} %get-tuple-element.168.mine_ref) | copy-start | bytes 3612676
  8.4 7.6 %copy-start.23 = (f32[48,3,384]{2,0,1:T(8,128)S(1)}, f32[48,3,384]{2,0,1:T(8,128)}, u32[]{:S(2)}) copy-start(f32[48,3,384]{2,0,1:T(8,128)} %param.28) | copy-start | bytes 663556
  8.4 90.9 %collective-permute-start = (bf16[784,768]{1,0:T(8,128)(2,1)S(1)}, bf16[784,768]{1,0:T(8,128)(2,1)S(1)}, u32[]{:S(2)}, u32[]{:S(2)}) collective-permute-start(bf16[784,768]{1,0:T(8,128)(2,1)S(1)} %get-tuple-element.168.mine_ref), channel_id=1, source_target_pairs={{0,1},{1,0},{2,3},{3,2},{4,5},{5,4},{6,7},{7,6},{8,9},{9,8},{10,11... | collective-permute-start | bytes 3612680 | tf_op jit(solution)/shard_map/ppermute | solution.py:659
  260.1 118.5 %collective-permute-start.1 = (bf16[784,768]{1,0:T(8,128)(2,1)}, bf16[784,768]{1,0:T(8,128)(2,1)S(1)}, u32[]{:S(2)}, u32[]{:S(2)}) collective-permute-start(bf16[784,768]{1,0:T(8,128)(2,1)} %get-tuple-element.70), channel_id=1, source_target_pairs={{0,1},{1,0},{2,3},{3,2},{4,5},{5,4},{6,7},{7,6},{8,9},{9,8},{10,11... | collective-permute-start | bytes 3612680 | tf_op jit(solution)/shard_map/ppermute | solution.py:666
  261.9 99.7 %copy-start.7 = (f32[48,1536]{1,0:T(8,128)S(1)}, f32[48,1536]{1,0:T(8,128)}, u32[]{:S(2)}) copy-start(f32[48,1536]{1,0:T(8,128)} %param.32) | copy-start | bytes 884740
  261.9 99.7 %copy-start.19 = (f32[48,1536]{1,0:T(8,128)S(1)}, f32[48,1536]{1,0:T(8,128)}, u32[]{:S(2)}) copy-start(f32[48,1536]{1,0:T(8,128)} %param.36) | copy-start | bytes 884740
  361.6 8.9 %copy-start.15 = (f32[48,384]{1,0:T(8,128)S(1)}, f32[48,384]{1,0:T(8,128)}, u32[]{:S(2)}) copy-start(f32[48,384]{1,0:T(8,128)} %param.29) | copy-start | bytes 221188
  361.6 8.9 %copy-start.30 = (f32[48,384]{1,0:T(8,128)S(1)}, f32[48,384]{1,0:T(8,128)}, u32[]{:S(2)}) copy-start(f32[48,384]{1,0:T(8,128)} %param.30) | copy-start | bytes 221188
  361.6 8.9 %copy-start.31 = (f32[48,384]{1,0:T(8,128)S(1)}, f32[48,384]{1,0:T(8,128)}, u32[]{:S(2)}) copy-start(f32[48,384]{1,0:T(8,128)} %param.31) | copy-start | bytes 221188
  361.6 17.1 %copy-start.27 = (f32[768]{0:T(1024)S(1)}, f32[768]{0:T(1024)}, u32[]{:S(2)}) copy-start(f32[768]{0:T(1024)} %param.21) | copy-start | bytes 9220
  361.6 17.0 %copy-start.29 = (f32[784]{0:T(1024)S(1)}, f32[784]{0:T(1024)}, u32[]{:S(2)}) copy-start(f32[784]{0:T(1024)} %copy-done.28) | copy-start | bytes 9412
  361.6 17.0 %copy-start.33 = (f32[768]{0:T(1024)S(1)}, f32[768]{0:T(1024)}, u32[]{:S(2)}) copy-start(f32[768]{0:T(1024)} %copy-done.32) | copy-start | bytes 9220
  361.7 17.0 %copy-start.35 = (f32[784]{0:T(1024)S(1)}, f32[784]{0:T(1024)}, u32[]{:S(2)}) copy-start(f32[784]{0:T(1024)} %copy-done.34) | copy-start | bytes 9412
  361.7 17.0 %copy-start.38 = (pred[784]{0:T(1024)(128)(4,1)S(1)}, pred[784]{0:T(1024)(128)(4,1)}, u32[]{:S(2)}) copy-start(pred[784]{0:T(1024)(128)(4,1)} %copy-done.37) | copy-start | bytes 2356
  367.6 11.1 %copy-start.2 = (f32[784,768]{1,0:T(8,128)S(1)}, f32[784,768]{1,0:T(8,128)}, u32[]{:S(2)}) copy-start(f32[784,768]{1,0:T(8,128)} %get-tuple-element.69) | copy-start | bytes 7225348
  384.7 53.4 %copy-start.18 = (f32[12,768]{1,0:T(8,128)S(1)}, f32[12,768]{1,0:T(8,128)}, u32[]{:S(2)}) copy-start(f32[12,768]{1,0:T(8,128)} %vec_ref.1) | copy-start | bytes 110596
  384.8 55.3 %copy-start.9 = (f32[48,1536]{1,0:T(8,128)S(1)}, f32[48,1536]{1,0:T(8,128)}, u32[]{:S(2)}) copy-start(f32[48,1536]{1,0:T(8,128)} %get-tuple-element.164) | copy-start | bytes 884740
  384.8 55.3 %copy-start.10 = (f32[48,1536]{1,0:T(8,128)S(1)}, f32[48,1536]{1,0:T(8,128)}, u32[]{:S(2)}) copy-start(f32[48,1536]{1,0:T(8,128)} %get-tuple-element.165) | copy-start | bytes 884740
  426.6 9.5 %copy-start.36 = (f32[12,768]{1,0:T(8,128)}, f32[12,768]{1,0:T(8,128)S(1)}, u32[]{:S(2)}) copy-start(f32[12,768]{1,0:T(8,128)S(1)} %get-tuple-element.145) | copy-start | bytes 110596
  (20 other events, 89.2 us)

commit v2 on v1

--- a/solution.py
+++ b/solution.py
@@ -59,106 +59,175 @@
     pl.semaphore_wait(barrier, 6)
 
 
-def gather_kernel(count, *refs):
-    shards, wholes = refs[:count], refs[count : 2 * count]
-    own_sem, send_sem, recv_sem = refs[2 * count :]
-    x, z, y, c = place()
-    lines, over_x, over_y, sibling = neighbours()
-    greet()
-
-    def remote(i, slot, src, dst, other):
+class Wires:
+    def __init__(self, send_sem, recv_sem):
+        self.send_sem, self.recv_sem = send_sem, recv_sem
+        self.started = []
+
+    def copy(self, slot, src, dst, other):
         return pltpu.make_async_remote_copy(
             src_ref=src,
             dst_ref=dst,
-            send_sem=send_sem.at[i, slot],
-            recv_sem=recv_sem.at[i, slot],
+            send_sem=self.send_sem.at[slot],
+            recv_sem=self.recv_sem.at[slot],
             device_id=other,
             device_id_type=MESH,
         )
 
-    def own(i):
-        return pltpu.make_async_copy(shards[i], wholes[i].at[x, z, y, c], own_sem.at[i])
-
-    def line(i, k):
-        return remote(i, k - 1, shards[i], wholes[i].at[x, z, y, c], lines[k - 1])
-
-    def plane(i, slot, other, part):
-        view = wholes[i].at[part]
-        return remote(i, slot, view, view, other)
-
-    def lane(i, k):
-        return (x, slice(None), y, c)
-
-    def step_two(i):
-        part = (x, slice(None), y, c)
-        return [plane(i, 3, over_x, part), plane(i, 4, over_y, part), plane(i, 7, sibling, part)]
-
-    def step_three(i):
-        return [
-            plane(i, 5, over_x, (x, pl.ds(0, 2), 1 - y, c)),
-            plane(i, 6, over_y, (1 - x, pl.ds(2, 2), y, c)),
-            plane(i, 8, sibling, (1 - x, slice(None), y, c)),
-            plane(i, 9, sibling, (x, slice(None), 1 - y, c)),
-        ]
-
-    def step_four(i):
-        return [plane(i, 10, sibling, (1 - x, slice(None), 1 - y, c))]
-
-    started = []
-
-    def start(copies):
-        for copy in copies:
-            copy.start()
-            started.append(copy)
-
-    for i in range(count):
-        own(i).start()
-        start([line(i, k) for k in (1, 2, 3)])
-    for turn in range(count + 2):
-        if turn < count:
-            i = turn
-            own(i).wait()
-            for k in (1, 2, 3):
-                line(i, k).wait_recv()
-            start(step_two(i))
-        if 0 <= turn - 1 < count:
-            i = turn - 1
-            two = step_two(i)
-            two[0].wait_recv()
-            two[1].wait_recv()
-            start(step_three(i))
-        if 0 <= turn - 2 < count:
-            i = turn - 2
-            three = step_three(i)
-            three[0].wait_recv()
-            three[1].wait_recv()
-            start(step_four(i))
-    for i in range(count):
-        step_two(i)[2].wait_recv()
-        step_three(i)[2].wait_recv()
-        step_three(i)[3].wait_recv()
-        step_four(i)[0].wait_recv()
-    for copy in started:
-        copy.wait_send()
-
-
-def gather_all(shards):
-    count = len(shards)
-    outs = [jax.ShapeDtypeStruct((2, 4, 2, 2, *s.shape), s.dtype) for s in shards]
-    wholes = pl.pallas_call(
-        functools.partial(gather_kernel, count),
-        out_shape=outs,
-        in_specs=[anywhere()] * count,
-        out_specs=[anywhere()] * count,
+    def start(self, slot, src, dst, other):
+        self.copy(slot, src, dst, other).start()
+        self.started.append((slot, src))
+
+    def send(self, slot, whole, part, other):
+        self.copy(slot, whole.at[part], whole.at[part], other).start()
+        self.started.append((slot, whole, part))
+
+    def arrive(self, slot, dst):
+        x, z, y, c = place()
+        self.copy(slot, dst, dst, device(x, z, y, 1 - c)).wait_recv()
+
+    def sent(self, slot, src):
+        x, z, y, c = place()
+        self.copy(slot, src, src, device(x, z, y, 1 - c)).wait_send()
+
+    def drain(self):
+        for slot, src, *part in self.started:
+            self.sent(slot, src.at[part[0]] if part else src)
+
+
+ALL = slice(None)
+
+
+def first_kernel(*refs):
+    (sa, sm, se, ss, patch_ref, mask_ref, token_ref, vec_ref) = refs[:8]
+    (wa_out, wm, we, ws, q_ref, k_ref, v_ref, a1_ref, other_ref) = refs[8:17]
+    wa, landing, own_sem, send_sem, recv_sem = refs[17:]
+    x, z, y, c = place()
+    lines, over_x, over_y, sibling = neighbours()
+    wires = Wires(send_sem, recv_sem)
+    rows = a1_ref.shape[0]
+    cut = rows // 32 * 16
+    halves = (pl.ds(0, cut), pl.ds(cut, rows - cut))
+    greet()
+
+    def back(k):
+        return lax.rem(z + 4 - k, 4)
+
+    own = [pltpu.make_async_copy(sa, wa.at[x, z, y, c], own_sem.at[0])]
+    for n, (shard, whole) in enumerate(((sm, wm), (se, we), (ss, ws))):
+        own.append(pltpu.make_async_copy(shard, whole.at[x, z, y, c], own_sem.at[n + 1]))
+    for copy in own:
+        copy.start()
+    for k in (1, 2, 3):
+        wires.start(k - 1, sa, wa.at[x, z, y, c], lines[k - 1])
+    wires.start(3, sa, wa.at[x, z, y, c], over_x)
+    wires.start(7, sa, wa.at[x, z, y, c], over_y)
+
+    tubes = jnp.where(mask_ref[...] > 0, token_ref[...], patch_ref[...].astype(F32))
+    centred = tubes - mean_rows(tubes)
+    scale = lax.rsqrt(mean_rows(centred * centred) + 1e-6)
+    a1_ref[...] = (centred * scale * vec_ref[0:1] + vec_ref[1:2]).astype(BF)
+    wires.start(19, a1_ref.at[halves[0]], landing.at[halves[0]], over_x)
+
+    for k in (1, 2, 3):
+        part = wa.at[x, back(k), y, c]
+        wires.arrive(k - 1, part)
+        wires.start(3 + k, part, part, over_x)
+        wires.start(7 + k, part, part, over_y)
+    wires.start(20, a1_ref.at[halves[1]], landing.at[halves[1]], over_x)
+    for copy in own:
+        copy.wait()
+    line = wa.at[x, ALL, y, c]
+    wires.start(15, line, line, sibling)
+    others = ((sm, wm), (se, we), (ss, ws))
+    for n, (shard, whole) in enumerate(others):
+        for k in (1, 2, 3):
+            wires.start(21 + 3 * n + k - 1, shard, whole.at[x, z, y, c], lines[k - 1])
+    for k in range(4):
+        part = wa.at[1 - x, back(k), y, c]
+        wires.arrive(3 + k, part)
+        wires.start(11 + k, part, part, over_y)
+    for n in range(2):
+        shard, whole = others[n]
+        wires.start(30 + 4 * n, shard, whole.at[x, z, y, c], over_y)
+    line = wa.at[1 - x, ALL, y, c]
+    wires.start(16, line, line, sibling)
+    for k in range(4):
+        wires.arrive(7 + k, wa.at[x, back(k), 1 - y, c])
+    line = wa.at[x, ALL, 1 - y, c]
+    wires.start(17, line, line, sibling)
+
+    def pass_on(n):
+        whole = others[n][1]
+        for k in (1, 2, 3):
+            part = whole.at[x, back(k), y, c]
+            wires.arrive(21 + 3 * n + k - 1, part)
+            wires.start(30 + 4 * n + k, part, part, over_y)
+
+    pass_on(0)
+    for k in range(4):
+        wires.arrive(11 + k, wa.at[1 - x, back(k), 1 - y, c])
+    line = wa.at[1 - x, ALL, 1 - y, c]
+    wires.start(18, line, line, sibling)
+    for n, (i, j) in enumerate(((x, y), (1 - x, y), (x, 1 - y), (1 - x, 1 - y))):
+        wires.arrive(15 + n, wa.at[i, ALL, j, 1 - c])
+    out_copy = pltpu.make_async_copy(wa, wa_out, own_sem.at[0])
+    out_copy.start()
+
+    width = wa.shape[-1] // 3
+    depth = a1_ref.shape[1]
+
+    def weight(h, n):
+        return wa[h, :, :, :, :, n * width : (n + 1) * width].reshape(depth, width)
+
+    def keys_values(h, source, span):
+        k_ref[h, span] = dot(source, weight(h, 1)).astype(BF)
+        values = dot(source, weight(h, 2)) + vec_ref[3:4, h * width : (h + 1) * width]
+        v_ref[h, span] = values.astype(BF)
+
+    for h in range(2):
+        queries = dot(a1_ref[...], weight(h, 0)) + vec_ref[2:3, h * width : (h + 1) * width]
+        q_ref[h] = (queries.astype(BF).astype(F32) * HD**-0.5).astype(BF)
+        keys_values(h, a1_ref[...], pl.ds(0, rows))
+    pass_on(1)
+    for n in range(2):
+        wires.arrive(19 + n, landing.at[halves[n]])
+        part = landing[halves[n]]
+        other_ref[halves[n]] = part
+        span = pl.ds(rows + (cut if n else 0), part.shape[0])
+        for h in range(2):
+            keys_values(h, part, span)
+    for n in range(2):
+        for k in range(4):
+            wires.arrive(30 + 4 * n + k, others[n][1].at[x, back(k), 1 - y, c])
+    for k in (1, 2, 3):
+        wires.arrive(27 + k - 1, ws.at[x, back(k), y, c])
+    out_copy.wait()
+    wires.drain()
+
+
+def first(shards, patches, mask, token, vectors):
+    rows, width = patches.shape
+    half = width // 2
+    gathered = [(2, 4, 2, 2, *s.shape) for s in shards]
+    wholes = [jax.ShapeDtypeStruct(g, BF) for g in gathered]
+    keys = jax.ShapeDtypeStruct((2, 2 * rows, half), BF)
+    flat = jax.ShapeDtypeStruct((rows, width), BF)
+    return pl.pallas_call(
+        first_kernel,
+        out_shape=[*wholes, jax.ShapeDtypeStruct((2, rows, half), BF), keys, keys, flat, flat],
+        in_specs=[anywhere()] * 4 + [in_vmem()] * 4,
+        out_specs=[anywhere()] * 4 + [in_vmem()] * 5,
         scratch_shapes=[
-            pltpu.SemaphoreType.DMA((count,)),
-            pltpu.SemaphoreType.DMA((count, 11)),
-            pltpu.SemaphoreType.DMA((count, 11)),
+            pltpu.VMEM(gathered[0], BF),
+            pltpu.VMEM((rows, width), BF),
+            pltpu.SemaphoreType.DMA((4,)),
+            pltpu.SemaphoreType.DMA((38,)),
+            pltpu.SemaphoreType.DMA((38,)),
         ],
         compiler_params=params(collective_id=0, has_side_effects=True),
-        name="gather_weights",
-    )(*shards)
-    return [w.reshape(2, -1, s.shape[-1]) for w, s in zip(wholes, shards)]
+        name="first",
+    )(*shards, patches, mask, token, vectors)
 
 
 def scatter_kernel(count, *refs):
@@ -300,19 +369,19 @@
     for h in range(2):
         cols = slice(h * half, (h + 1) * half)
         queries = dot(mine_ref[...], w_ref[h, :, :half]) + bias_ref[0:1, cols]
-        q_ref[:, cols] = (queries.astype(BF).astype(F32) * HD**-0.5).astype(BF)
+        q_ref[h] = (queries.astype(BF).astype(F32) * HD**-0.5).astype(BF)
         for part, ref in ((0, mine_ref), (1, other_ref)):
             span = slice(part * rows, (part + 1) * rows)
-            k_ref[span, cols] = dot(ref[...], w_ref[h, :, half : 2 * half]).astype(BF)
-            v_ref[span, cols] = (dot(ref[...], w_ref[h, :, 2 * half :]) + bias_ref[1:2, cols]).astype(BF)
+            k_ref[h, span] = dot(ref[...], w_ref[h, :, half : 2 * half]).astype(BF)
+            v_ref[h, span] = (dot(ref[...], w_ref[h, :, 2 * half :]) + bias_ref[1:2, cols]).astype(BF)
 
 
 def project(mine, other, weight, bias):
     rows, width = mine.shape
-    keys = jax.ShapeDtypeStruct((2 * rows, width), BF)
+    keys = jax.ShapeDtypeStruct((2, 2 * rows, width // 2), BF)
     return pl.pallas_call(
         project_kernel,
-        out_shape=[jax.ShapeDtypeStruct((rows, width), BF), keys, keys],
+        out_shape=[jax.ShapeDtypeStruct((2, rows, width // 2), BF), keys, keys],
         in_specs=[in_vmem()] * 4,
         out_specs=[in_vmem()] * 3,
         compiler_params=params(),
@@ -325,48 +394,133 @@
     return lane < HD, lane >= HD
 
 
-def attend_kernel(q_ref, k_ref, v_ref, o_ref, low_ref, p_ref):
-    sides = half_lanes()
-    q, k, v = q_ref[...], k_ref[...], v_ref[...]
-    outs = []
-    for h in range(2):
-        s = dot(jnp.where(sides[h], q, jnp.zeros_like(q)), k, NT)
-        top = jnp.max(s, axis=-1, keepdims=True)
-        e = jnp.exp2(s * LOG2E - top * LOG2E)
-        total = jnp.sum(e, axis=-1, keepdims=True)
-        p = (e * (1.0 / total)).astype(BF)
-        p_ref[h] = p
-        outs.append(dot(p, v))
-    o = jnp.where(sides[0], outs[0], outs[1])
-    o_ref[...] = o
-    low_ref[...] = o.astype(BF)
-
-
-def attend(q, k, v):
-    rows, width = q.shape
-    keys = k.shape[0]
-    pairs = width // PAIR
-    of_q = pl.BlockSpec((rows, PAIR), lambda i: (0, i))
-    of_k = pl.BlockSpec((keys, PAIR), lambda i: (0, i))
+def attend_head(h, q, k, v, p_ref):
+    s = dot(jnp.where(half_lanes()[h], q, jnp.zeros_like(q)), k, NT)
+    top = jnp.max(s, axis=-1, keepdims=True)
+    e = jnp.exp2(s * LOG2E - top * LOG2E)
+    total = jnp.sum(e, axis=-1, keepdims=True)
+    p = (e * (1.0 / total)).astype(BF)
+    p_ref[h] = p
+    return dot(p, v)
+
+
+def attend_plain_kernel(q_ref, k_ref, v_ref, o_ref, low_ref, p_ref):
+    q, k, v = q_ref[0], k_ref[0], v_ref[0]
+    o = jnp.where(half_lanes()[0], *(attend_head(h, q, k, v, p_ref) for h in range(2)))
+    o_ref[0] = o
+    low_ref[0] = o.astype(BF)
+
+
+def attend_kernel(*refs):
+    q_ref, k_ref, v_ref = refs[:3]
+    o_ref, low_ref, p_ref, wm, we, ws, send_sem, recv_sem = refs[6:]
+    i = pl.program_id(0)
+    x, z, y, c = place()
+    lines, over_x, over_y, sibling = neighbours()
+    wires = Wires(send_sem, recv_sem)
+    here, side, flank, across = (x, ALL, y, c), (1 - x, ALL, y, c), (x, ALL, 1 - y, c), (1 - x, ALL, 1 - y, c)
+
+    send = wires.send
+
+    @pl.when(i == 0)
+    def _():
+        greet()
+        send(0, wm, here, over_x)
+        send(1, we, here, over_x)
+        send(2, ws, here, over_y)
+        send(3, ws, here, over_x)
+        send(4, wm, flank, over_x)
+        send(5, wm, here, sibling)
+        send(6, wm, flank, sibling)
+        send(7, we, here, sibling)
+        send(8, we, flank, sibling)
+        send(9, ws, here, sibling)
+
+    @pl.when(i == 2)
+    def _():
+        wires.arrive(0, wm.at[side])
+        send(10, wm, side, sibling)
+        wires.arrive(1, we.at[side])
+        send(11, we, side, over_y)
+        send(12, we, side, sibling)
+
+    @pl.when(i == 4)
+    def _():
+        wires.arrive(3, ws.at[side])
+        send(13, ws, side, over_y)
+        send(14, ws, side, sibling)
+        wires.arrive(2, ws.at[flank])
+        send(15, ws, flank, sibling)
+        wires.arrive(4, wm.at[across])
+        send(16, wm, across, sibling)
+
+    q, k, v = q_ref[0], k_ref[0], v_ref[0]
+    o = jnp.where(half_lanes()[0], *(attend_head(h, q, k, v, p_ref) for h in range(2)))
+    o_ref[0] = o
+    low_ref[0] = o.astype(BF)
+
+    @pl.when(i == pl.num_programs(0) - 1)
+    def _():
+        wires.arrive(11, we.at[across])
+        send(17, we, across, sibling)
+        wires.arrive(13, ws.at[across])
+        send(18, ws, across, sibling)
+        for slot, whole, (a, b) in (
+            (5, wm, (x, y)),
+            (6, wm, (x, 1 - y)),
+            (7, we, (x, y)),
+            (8, we, (x, 1 - y)),
+            (9, ws, (x, y)),
+            (10, wm, (1 - x, y)),
+            (12, we, (1 - x, y)),
+            (14, ws, (1 - x, y)),
+            (15, ws, (x, 1 - y)),
+            (16, wm, (1 - x, 1 - y)),
+            (17, we, (1 - x, 1 - y)),
+            (18, ws, (1 - x, 1 - y)),
+        ):
+            wires.arrive(slot, whole.at[a, ALL, b, 1 - c])
+        wires.drain()
+
+
+def attend(q, k, v, wholes):
+    _, rows, half = q.shape
+    keys = k.shape[1]
+    per = half // PAIR
+    of_q = pl.BlockSpec((1, rows, PAIR), lambda i: (i // per, 0, lax.rem(i, per)))
+    of_k = pl.BlockSpec((1, keys, PAIR), lambda i: (i // per, 0, lax.rem(i, per)))
+    shapes = [
+        jax.ShapeDtypeStruct(q.shape, F32),
+        jax.ShapeDtypeStruct(q.shape, BF),
+        jax.ShapeDtypeStruct((4 * per, rows, keys), BF),
+    ]
+    of_p = pl.BlockSpec((2, rows, keys), lambda i: (i, 0, 0))
+    common = dict(grid=(2 * per,), name="attend")
+    if not wholes:
+        return pl.pallas_call(
+            attend_plain_kernel,
+            in_specs=[of_q, of_k, of_k],
+            out_specs=[of_q, of_q, of_p],
+            out_shape=shapes,
+            compiler_params=params(),
+            **common,
+        )(q, k, v)
     return pl.pallas_call(
         attend_kernel,
-        grid=(pairs,),
-        in_specs=[of_q, of_k, of_k],
-        out_specs=[of_q, of_q, pl.BlockSpec((2, rows, keys), lambda i: (i, 0, 0))],
-        out_shape=[
-            jax.ShapeDtypeStruct((rows, width), F32),
-            jax.ShapeDtypeStruct((rows, width), BF),
-            jax.ShapeDtypeStruct((2 * pairs, rows, keys), BF),
-        ],
-        compiler_params=params(),
-        name="attend",
-    )(q, k, v)
+        in_specs=[of_q, of_k, of_k, *[anywhere()] * 3],
+        out_specs=[of_q, of_q, of_p, *[anywhere()] * 3],
+        out_shape=[*shapes, *[jax.ShapeDtypeStruct(w.shape, BF) for w in wholes]],
+        input_output_aliases={3: 3, 4: 4, 5: 5},
+        scratch_shapes=[pltpu.SemaphoreType.DMA((19,)), pltpu.SemaphoreType.DMA((19,))],
+        compiler_params=params(collective_id=2, has_side_effects=True),
+        **common,
+    )(q, k, v, *wholes)
 
 
 def attend_back_kernel(q_ref, k_ref, v_ref, do_ref, o_ref, p_ref, dq_ref, dk_ref, dv_ref):
     sides = half_lanes()
-    q, k, v, do = q_ref[...], k_ref[...], v_ref[...], do_ref[...]
-    prod = do.astype(F32) * o_ref[...]
+    q, k, v, do = q_ref[0], k_ref[0], v_ref[0], do_ref[0]
+    prod = do.astype(F32) * o_ref[0]
     outs, grad_k, grad_v = [], None, None
     for h in range(2):
         do_h = jnp.where(sides[h], do, jnp.zeros_like(do))
@@ -379,26 +533,26 @@
         more_k, more_v = dot(ds, q_h, TN), dot(p, do_h, TN)
         grad_k = more_k if grad_k is None else grad_k + more_k
         grad_v = more_v if grad_v is None else grad_v + more_v
-    dq_ref[...] = (jnp.where(sides[0], outs[0], outs[1]) * HD**-0.5).astype(BF)
-    dk_ref[...] = grad_k.astype(BF)
-    dv_ref[...] = grad_v.astype(BF)
+    dq_ref[0] = (jnp.where(sides[0], outs[0], outs[1]) * HD**-0.5).astype(BF)
+    dk_ref[0] = grad_k.astype(BF)
+    dv_ref[0] = grad_v.astype(BF)
 
 
 def attend_back(q, k, v, do, o, p):
-    rows, width = q.shape
-    keys = k.shape[0]
-    pairs = width // PAIR
-    of_q = pl.BlockSpec((rows, PAIR), lambda i: (0, i))
-    of_k = pl.BlockSpec((keys, PAIR), lambda i: (0, i))
+    _, rows, half = q.shape
+    keys = k.shape[1]
+    per = half // PAIR
+    of_q = pl.BlockSpec((1, rows, PAIR), lambda i: (i // per, 0, lax.rem(i, per)))
+    of_k = pl.BlockSpec((1, keys, PAIR), lambda i: (i // per, 0, lax.rem(i, per)))
     return pl.pallas_call(
         attend_back_kernel,
-        grid=(pairs,),
+        grid=(2 * per,),
         in_specs=[of_q, of_k, of_k, of_q, of_q, pl.BlockSpec((2, rows, keys), lambda i: (i, 0, 0))],
         out_specs=[of_q, of_k, of_k],
         out_shape=[
-            jax.ShapeDtypeStruct((rows, width), BF),
-            jax.ShapeDtypeStruct((keys, width), BF),
-            jax.ShapeDtypeStruct((keys, width), BF),
+            jax.ShapeDtypeStruct(q.shape, BF),
+            jax.ShapeDtypeStruct(k.shape, BF),
+            jax.ShapeDtypeStruct(k.shape, BF),
         ],
         compiler_params=params(),
         name="attend_back",
@@ -422,7 +576,9 @@
 
 
 def middle_kernel(
-    x_ref,
+    patch_ref,
+    mask_ref,
+    token_ref,
     o_ref,
     dy_ref,
     vec_ref,
@@ -444,13 +600,12 @@
     da2_ref,
 ):
     i = pl.program_id(0)
-    half = wm_ref.shape[2]
 
     @pl.when(i == 0)
     def _():
-        x1 = x_ref[...] + vec_ref[4:5]
+        x1 = jnp.where(mask_ref[...] > 0, token_ref[...], patch_ref[...].astype(F32)) + vec_ref[4:5]
         for h in range(2):
-            x1 = x1 + dot(o_ref[:, h * half : (h + 1) * half], wm_ref[h], NT)
+            x1 = x1 + dot(o_ref[h], wm_ref[h], NT)
         x1_ref[...] = x1
         centred = x1 - mean_rows(x1)
         scale = lax.rsqrt(mean_rows(centred * centred) + 1e-6)
@@ -485,9 +640,8 @@
         dx1_ref[...] = dx1
         dxb = dx1.astype(BF)
         for h in range(2):
-            cols = slice(h * half, (h + 1) * half)
-            do_ref[:, cols] = dot(dxb, wm_ref[h]).astype(BF)
-            gm_ref[h] = dot(dxb, o_ref[:, cols], TN).astype(BF)
+            do_ref[h] = dot(dxb, wm_ref[h]).astype(BF)
+            gm_ref[h] = dot(dxb, o_ref[h], TN).astype(BF)
         gv_ref[0:1] = jnp.sum(dxb.astype(F32), axis=0, keepdims=True)
         gv_ref[1:2] = jnp.sum(da2 * xh, axis=0, keepdims=True)
         gv_ref[2:3] = jnp.sum(da2, axis=0, keepdims=True)
@@ -495,8 +649,8 @@
         gv_ref[4:] = jnp.zeros((4, gv_ref.shape[1]), F32)
 
 
-def middle(x, o, dy, vectors, wm, we, ws):
-    rows, width = x.shape
+def middle(patches, mask, token, o, dy, vectors, wm, we, ws):
+    rows, width = patches.shape
     hidden = we.shape[2]
     block = 512
     per = hidden // block
@@ -512,7 +666,9 @@
         grid=(steps,),
         in_specs=[
             whole((rows, width)),
-            whole((rows, width)),
+            whole((rows, 1)),
+            whole((1, width)),
+            whole(o.shape),
             whole((rows, width)),
             whole(vectors.shape),
             of_u,
@@ -523,7 +679,7 @@
         out_specs=[
             whole((rows, width)),
             whole((rows, width)),
-            whole((rows, width)),
+            whole(o.shape),
             whole(wm.shape),
             of_w,
             of_w,
@@ -533,7 +689,7 @@
         out_shape=[
             jax.ShapeDtypeStruct((rows, width), BF),
             jax.ShapeDtypeStruct((rows, width), F32),
-            jax.ShapeDtypeStruct((rows, width), BF),
+            jax.ShapeDtypeStruct(o.shape, BF),
             jax.ShapeDtypeStruct(wm.shape, BF),
             jax.ShapeDtypeStruct(we.shape, BF),
             jax.ShapeDtypeStruct(ws.shape, BF),
@@ -548,7 +704,7 @@
         ],
         compiler_params=params(),
         name="middle",
-    )(x, o, dy, vectors, vectors[7:11].reshape(1, -1), wm, we, ws)
+    )(patches, mask, token, o, dy, vectors, vectors[7:11].reshape(1, -1), wm, we, ws)
 
 
 def unproject_kernel(
@@ -560,8 +716,7 @@
     gv_ref[...] = jnp.zeros_like(gv_ref)
     for h in range(2):
         cols = slice(h * half, (h + 1) * half)
-        dq = dq_ref[:, cols]
-        dk, dv = dk_ref[:, cols], dv_ref[:, cols]
+        dq, dk, dv = dq_ref[h], dk_ref[h], dv_ref[h]
         wq, wk, wv = (w_ref[h, :, n * half : (n + 1) * half] for n in range(3))
         mine = dot(dq, wq, NT) + dot(dk[:rows], wk, NT) + dot(dv[:rows], wv, NT)
         other = dot(dk[rows:], wk, NT) + dot(dv[rows:], wv, NT)
@@ -644,23 +799,28 @@
         shrink_master,
     ]
     shards = [m.astype(BF) for m in masters]
+    swap = [(0, 1), (1, 0)]
+    mask, token, dy = cube_mask.reshape(rows, 1), mask_token[None], cotangent[0]
+    chosen = mask > 0
+    x = jnp.where(chosen, token, patches[0].astype(F32))
+    centred = x - mean_rows(x)
+    scale = lax.rsqrt(mean_rows(centred * centred) + 1e-6)
     if direct:
-        wa, wm, we, ws = gather_all(shards)
+        *wholes, q, k, v, a1, a1_other = first(shards, patches[0], mask, token, vectors)
+        wa = wholes[0].reshape(2, width, -1)
+        o, o_low, p, *rest = attend(q, k, v, wholes[1:])
+        wm, we, ws = (w.reshape(2, width, -1) for w in rest)
     else:
         wa, wm, we, ws = (
             lax.all_gather(lax.all_gather(s, "dp", axis=0, tiled=True), "mp", axis=0) for s in shards
         )
-    swap = [(0, 1), (1, 0)]
-    chosen = cube_mask[0, :, None] > 0
-    x = jnp.where(chosen, mask_token, patches[0].astype(F32))
-    centred = x - mean_rows(x)
-    scale = lax.rsqrt(mean_rows(centred * centred) + 1e-6)
-    a1 = (centred * scale * vectors[0] + vectors[1]).astype(BF)
-    a1_other = lax.ppermute(a1, "mp", swap)
-    q, k, v = project(a1, a1_other, wa, vectors[2:4])
-    o, o_low, p = attend(q, k, v)
-    dy = cotangent[0]
-    block_out, dx1, do, gm, ge, gs, gu, gv = middle(x, o_low, dy, vectors, wm, we, ws)
+        a1 = (centred * scale * vectors[0] + vectors[1]).astype(BF)
+        a1_other = lax.ppermute(a1, "mp", swap)
+        q, k, v = project(a1, a1_other, wa, vectors[2:4])
+        o, o_low, p = attend(q, k, v, [])
+    block_out, dx1, do, gm, ge, gs, gu, gv = middle(
+        patches[0], mask, token, o_low, dy, vectors, wm, we, ws
+    )
     dq, dk, dv = attend_back(q, k, v, do, o, p)
     da1, da1_send, ga, gqv = unproject(a1, a1_other, dq, dk, dv, wa)
     da1 = da1 + lax.ppermute(da1_send, "mp", swap).astype(F32)

time: 450 us -> 416 us (0.924)
  Pallas kernels: 340 us -> 310 us
  local copies, waits for them, and re-layouts: 10.6 us -> 16.8 us
  other arithmetic: 38.6 us -> 32.6 us
    pallas_call x4 -> x3, Pallas kernels: 175 us -> 153 us  [the longest x1 56.2 us: first(): pl.pallas_call(first_kernel, out_shape=[*wholes, jax.ShapeDtypeStruct((2,...]
    pallas_call x1, Pallas kernels: 99.7 us -> 91.5 us  [scatter_all(): pl.pallas_call(functools.partial(scatter_kernel, count), out_shape=[jax.S...]
  transfers between devices with their start and end apart: 2 -> 1, of which waited for: 0 -> 0; matrix products, arithmetic and copies ran while one was open for 5% -> 5% of each run, Pallas kernels for 41% -> 22%
where the time goes in v2:
time: 416 us; the launch traced here: 410 us
  Pallas kernels  310 us (75%)
  blocking collectives  42.1 us (10%)
  other arithmetic  32.6 us (8%)
  local copies, waits for them, and re-layouts  16.8 us (4%)
  between operations  6.67 us (2%)
    pallas_call x1, Pallas kernels, scatter_all(): pl.pallas_call(functools.partial(scatter_kernel, count), out_shape=[jax.S...  91.5 us
    pallas_call x1, Pallas kernels, first(): pl.pallas_call(first_kernel, out_shape=[*wholes, jax.ShapeDtypeStruct((2,...  56.2 us
    pallas_call x1, Pallas kernels, attend(): pl.pallas_call(attend_kernel, in_specs=[of_q, of_k, of_k, *[anywhere()] *...  55.5 us
    pallas_call x1, Pallas kernels, middle(): pl.pallas_call(middle_kernel, grid=(steps,), in_specs=[whole((rows, width...  45.5 us
    psum x1, blocking collectives, per_device(): lax.psum((vector_part, token_part, squares), ('dp', 'mp'))  42.1 us
    pallas_call x1, Pallas kernels, attend_back(): pl.pallas_call(attend_back_kernel, grid=(2 * per,), in_specs=[of_q, of_k,...  41 us
    pallas_call x1, Pallas kernels, unproject(): pl.pallas_call(unproject_kernel, out_shape=[jax.ShapeDtypeStruct((rows, w...  20.4 us
  transfers between devices with their start and end apart: 1, of which 0 were waited for; matrix products, arithmetic and copies ran while one was open for 5% of the time, Pallas kernels for 22%

profile of v2, /device:TPU:0, one launch (start us, length us, event | category | flops | bytes accessed | tf_op | source)
XLA Modules:
  0.0 409.9 jit_solution(8855769125631163183)
XLA Ops:
  2.3 1.6 copy.56.refs_5_.mask_ref
  3.9 1.3 broadcast_in_dim.55.refs_6_.token_ref
  5.2 1.6 convert_element_type.35.refs_2_
  6.8 1.6 convert_element_type.36.refs_3_
  8.5 1.5 convert_element_type.34.refs_1_
  11.4 56.2 %first.1 = (bf16[2,4,2,2,48,1152]{5,4,3,2,1,0:T(8,128)(2,1)}, bf16[2,4,2,2,48,384]{5,4,3,2,1,0:T(8,128)(2,1)}, bf16[2,4,2,2,48,1536]{5,4,3,2,1,0:T(8,128)(2,1)},...) custom-call(bf16[48,1152]{1,0:T(8,128)(2,1)} %convert_element_type.3, ...), custom_call_target="tpu_custom_call" | custom-call | tf_op jit(solution)/shard_map/first/pallas_call | solution.py:216
  67.6 55.5 %attend.1 = (f32[2,784,384]{2,1,0:T(8,128)}, bf16[2,784,384]{2,1,0:T(8,128)(2,1)}, bf16[12,784,1568]{2,1,0:T(8,128)(2,1)}, bf16[2,4,2,2,48,384]{5,4,3,2,1,0:T(8,...) custom-call(bf16[2,784,384]{2,1,0:T(8,128)(2,1)} %get-tuple-element., ...), custom_call_target="tpu_custom_call", output_to_operand_aliasing={{3}: (3, {}), {4}: (4, {}), {5}: (5, {})} | custom-call | tf_op jit(solution)/shard_map/attend/pallas_call | solution.py:508
  123.1 45.5 %middle.1 = (bf16[784,768]{1,0:T(8,128)(2,1)}, f32[784,768]{1,0:T(8,128)}, bf16[2,784,384]{2,1,0:T(8,128)(2,1)}, bf16[2,768,384]{2,1,0:T(8,128)(2,1)}, bf16[2,76...) custom-call(bf16[784,768]{1,0:T(8,128)(2,1)} %bitcast.67, ...), custom_call_target="tpu_custom_call" | custom-call | tf_op jit(solution)/shard_map/middle/pallas_call | solution.py:664
  168.6 41.0 %attend_back.1 = (bf16[2,784,384]{2,1,0:T(8,128)(2,1)}, bf16[2,1568,384]{2,1,0:T(8,128)(2,1)}, bf16[2,1568,384]{2,1,0:T(8,128)(2,1)}) custom-call(bf16[2,784,384]{2,1,0:T(8,128)(2,1)} %get-tuple-element.58.refs_0_.q_ref, bf16[2,1568,384]{2,1,0:T(8,128)(2,1)} %get-tuple-element.59.refs_1_.k_ref, bf16[2,1568,384]{2,1,0:T(8,128)(2,1)} %get-tuple-element.60.refs_2_.v_ref, ...), custom_call_target="tpu_custom_call" | custom-call | tf_op jit(solution)/shard_map/attend_back/pallas_call | solution.py:547
  209.7 20.4 %unproject.1 = (f32[784,768]{1,0:T(8,128)}, bf16[784,768]{1,0:T(8,128)(2,1)}, bf16[2,768,1152]{2,1,0:T(8,128)(2,1)}, f32[8,768]{1,0:T(8,128)}) custom-call(bf16[784,768]{1,0:T(8,128)(2,1)} %get-tuple-element.70.mine_ref, bf16[784,768]{1,0:T(8,128)(2,1)} %get-tuple-element.71.other_ref, bf16[2,784,384]{2,1,0:T(8,128)(2,1)} %get-tuple-element.75.dq_ref, ...), custom_call_target="tpu_custom_call" | custom-call | tf_op jit(solution)/shard_map/unproject/pallas_call | solution.py:737
  230.2 1.5 collective-permute-start
  235.3 1.3 slice.64
  238.4 91.5 %scatter_grads.1 = (f32[48,1152]{1,0:T(8,128)}, f32[48,384]{1,0:T(8,128)}, f32[48,1536]{1,0:T(8,128)}, f32[48,1536]{1,0:T(8,128)}) custom-call(bf16[2,4,2,2,48,1152]{5,4,3,2,1,0:T(8,128)(2,1)} %bitcast.73, bf16[2,4,2,2,48,384]{5,4,3,2,1,0:T(8,128)(2,1)} %bitcast.81, bf16[2,4,2,2,48,1536]{5,4,3,2,1,0:T(8,128)(2,1)} %bitcast.70, ...), custom_call_target="tpu_custom_call" | custom-call | tf_op jit(solution)/shard_map/scatter_grads/pallas_call | solution.py:346
  330.1 3.5 multiply_reduce_fusion.5
  333.6 1.4 maximum_bitcast_fusion.2
  335.0 1.4 maximum_bitcast_fusion.3
  337.1 1.3 multiply_reduce_fusion.11
  338.5 2.7 maximum_bitcast_fusion
  343.7 1.6 multiply_reduce_fusion
  345.9 2.3 concatenate.3
  348.2 4.1 %select_reduce_fusion = (f32[768]{0:T(1024)}, bf16[784,768]{1,0:T(8,128)(2,1)S(1)}) fusion(pred[784]{0:T(1024)(128)(4,1)} %copy-done.30, f32[784,768]{1,0:T(8,128)} %get-tuple-element.69, f32[784]{0:T(1024)} %get-tuple-element.184, f32[784]{0:T(1024)S(1)} %broadcast_multiply_fusion.2, bf16[1,784,768]{2,1,0:T(8,128)(2,1)S(1)} %copy-done, ...), kind=kLoop, calls=%fused_computation.1 | loop fusion | flops 9030912 | bytes 8452112 | tf_op jit(solution)/shard_map/reduce_sum | solution.py:841
  352.3 42.1 %all-reduce = (f32[768]{0:T(1024)}, f32[12,768]{1,0:T(8,128)S(1)}, f32[4,2]{1,0:T(4,128)S(1)}) all-reduce(f32[768]{0:T(1024)} %get-tuple-element.174, f32[12,768]{1,0:T(8,128)S(1)} %concatenate.3, f32[4,2]{1,0:T(4,128)} %pad_maximum_fusion), channel_id=1, replica_groups=mesh['dp'=16,'mp'=2] {'dp','mp'}, use_global_device_ids=true, to_apply=%region_5.6 | all-reduce | flops 9992 | bytes 79936 | tf_op jit(solution)/shard_map/psum | solution.py:863
  400.9 1.1 fusion.14
  404.0 2.0 fusion.3
  (107 shorter events, 19.1 us)
Async XLA Ops:
  209.6 22.0 %copy-start.11 = (f32[48,3,384]{2,0,1:T(8,128)S(1)}, f32[48,3,384]{2,0,1:T(8,128)}, u32[]{:S(2)}) copy-start(f32[48,3,384]{2,0,1:T(8,128)} %param.26) | copy-start | bytes 663556
  209.7 22.9 %copy-start.31 = (s32[1,784]{1,0:T(1,128)S(1)}, s32[1,784]{1,0:T(1,128)}, u32[]{:S(2)}) copy-start(s32[1,784]{1,0:T(1,128)} %param.20) | copy-start | bytes 9412
  209.7 22.9 %copy-start.10 = (f32[12,768]{1,0:T(8,128)S(1)}, f32[12,768]{1,0:T(8,128)}, u32[]{:S(2)}) copy-start(f32[12,768]{1,0:T(8,128)} %vec_ref.1) | copy-start | bytes 110596
  209.7 23.0 %copy-start.33 = (f32[8,768]{1,0:T(8,128)S(1)}, f32[8,768]{1,0:T(8,128)}, u32[]{:S(2)}) copy-start(f32[8,768]{1,0:T(8,128)} %get-tuple-element.82) | copy-start | bytes 73732
  209.7 24.1 %copy-start.19 = (f32[48,3,384]{2,0,1:T(8,128)S(1)}, f32[48,3,384]{2,0,1:T(8,128)}, u32[]{:S(2)}) copy-start(f32[48,3,384]{2,0,1:T(8,128)} %param.27) | copy-start | bytes 663556
  209.7 24.9 %copy-start.20 = (f32[48,3,384]{2,0,1:T(8,128)S(1)}, f32[48,3,384]{2,0,1:T(8,128)}, u32[]{:S(2)}) copy-start(f32[48,3,384]{2,0,1:T(8,128)} %param.28) | copy-start | bytes 663556
  209.7 27.4 %copy-start.32 = (f32[1,3072]{1,0:T(1,128)S(1)}, f32[1,3072]{1,0:T(1,128)}, u32[]{:S(2)}) copy-start(f32[1,3072]{1,0:T(1,128)} %get-tuple-element.83) | copy-start | bytes 36868
  230.2 113.5 %collective-permute-start = (bf16[784,768]{1,0:T(8,128)(2,1)}, bf16[784,768]{1,0:T(8,128)(2,1)S(1)}, u32[]{:S(2)}, u32[]{:S(2)}) collective-permute-start(bf16[784,768]{1,0:T(8,128)(2,1)} %get-tuple-element.80), channel_id=1, source_target_pairs={{0,1},{1,0},{2,3},{3,2},{4,5},{5,4},{6,7},{7,6},{8,9},{9,8},{10,11... | collective-permute-start | bytes 3612680 | tf_op jit(solution)/shard_map/ppermute | solution.py:826
  232.6 111.1 %copy-start.30 = (pred[784]{0:T(1024)(128)(4,1)}, pred[784]{0:T(1024)(128)(4,1)S(1)}, u32[]{:S(2)}) copy-start(pred[784]{0:T(1024)(128)(4,1)S(1)} %compare_reduce_fusion) | copy-start | bytes 2356
  238.4 91.5 %copy-start.3 = (f32[48,1536]{1,0:T(8,128)S(1)}, f32[48,1536]{1,0:T(8,128)}, u32[]{:S(2)}) copy-start(f32[48,1536]{1,0:T(8,128)} %param.35) | copy-start | bytes 884740
  238.4 91.5 %copy-start.4 = (f32[48,1536]{1,0:T(8,128)S(1)}, f32[48,1536]{1,0:T(8,128)}, u32[]{:S(2)}) copy-start(f32[48,1536]{1,0:T(8,128)} %param.32) | copy-start | bytes 884740
  238.4 91.6 %copy-start.16 = (f32[48,1536]{1,0:T(8,128)S(1)}, f32[48,1536]{1,0:T(8,128)}, u32[]{:S(2)}) copy-start(f32[48,1536]{1,0:T(8,128)} %param.36) | copy-start | bytes 884740
  330.0 7.1 %copy-start.14 = (f32[48,384]{1,0:T(8,128)S(1)}, f32[48,384]{1,0:T(8,128)}, u32[]{:S(2)}) copy-start(f32[48,384]{1,0:T(8,128)} %param.29) | copy-start | bytes 221188
  330.0 7.1 %copy-start.25 = (f32[48,384]{1,0:T(8,128)S(1)}, f32[48,384]{1,0:T(8,128)}, u32[]{:S(2)}) copy-start(f32[48,384]{1,0:T(8,128)} %param.30) | copy-start | bytes 221188
  330.0 7.1 %copy-start.26 = (f32[48,384]{1,0:T(8,128)S(1)}, f32[48,384]{1,0:T(8,128)}, u32[]{:S(2)}) copy-start(f32[48,384]{1,0:T(8,128)} %param.31) | copy-start | bytes 221188
  330.0 7.1 %copy-start.27 = (f32[48,384]{1,0:T(8,128)S(1)}, f32[48,384]{1,0:T(8,128)}, u32[]{:S(2)}) copy-start(f32[48,384]{1,0:T(8,128)} %get-tuple-element.89) | copy-start | bytes 221188
  330.0 11.7 %copy-start = (bf16[1,784,768]{2,1,0:T(8,128)(2,1)S(1)}, bf16[1,784,768]{2,1,0:T(8,128)(2,1)}, u32[]{:S(2)}) copy-start(bf16[1,784,768]{2,1,0:T(8,128)(2,1)} %param.19) | copy-start | bytes 3612676
  330.0 11.7 %copy-start.24 = (f32[768]{0:T(1024)S(1)}, f32[768]{0:T(1024)}, u32[]{:S(2)}) copy-start(f32[768]{0:T(1024)} %param.21) | copy-start | bytes 9220
  336.3 7.4 %copy-start.1 = (f32[784,768]{1,0:T(8,128)S(1)}, f32[784,768]{1,0:T(8,128)}, u32[]{:S(2)}) copy-start(f32[784,768]{1,0:T(8,128)} %get-tuple-element.79) | copy-start | bytes 7225348
  337.1 6.6 %copy-start.5 = (f32[48,1152]{1,0:T(8,128)}, f32[48,1152]{1,0:T(8,128)S(1)}, u32[]{:S(2)}) copy-start(f32[48,1152]{1,0:T(8,128)S(1)} %get-tuple-element.167) | copy-start | bytes 663556
  352.3 53.7 %copy-start.28 = (f32[12,768]{1,0:T(8,128)S(1)}, f32[12,768]{1,0:T(8,128)}, u32[]{:S(2)}) copy-start(f32[12,768]{1,0:T(8,128)} %param.25) | copy-start | bytes 110596
  352.3 53.7 %copy-start.29 = (f32[12,768]{1,0:T(8,128)S(1)}, f32[12,768]{1,0:T(8,128)}, u32[]{:S(2)}) copy-start(f32[12,768]{1,0:T(8,128)} %param.24) | copy-start | bytes 110596
  352.3 54.7 %copy-start.6 = (f32[48,1536]{1,0:T(8,128)S(1)}, f32[48,1536]{1,0:T(8,128)}, u32[]{:S(2)}) copy-start(f32[48,1536]{1,0:T(8,128)} %get-tuple-element.172) | copy-start | bytes 884740
  352.3 54.7 %copy-start.7 = (f32[48,1536]{1,0:T(8,128)S(1)}, f32[48,1536]{1,0:T(8,128)}, u32[]{:S(2)}) copy-start(f32[48,1536]{1,0:T(8,128)} %get-tuple-element.173) | copy-start | bytes 884740
  (11 other events, 54.5 us)

commit v3 on v2

--- a/solution.py
+++ b/solution.py
@@ -230,137 +230,8 @@
     )(*shards, patches, mask, token, vectors)
 
 
-def scatter_kernel(count, *refs):
-    grads, totals = refs[:count], refs[count : 2 * count]
-    refs = refs[2 * count :]
-    mine, sib, diag, side, far = (refs[k * count : (k + 1) * count] for k in range(5))
-    own_sem, send_sem, recv_sem = refs[5 * count :]
-    x, z, y, c = place()
-    lines, over_x, over_y, sibling = neighbours()
-    greet()
-
-    def remote(i, slot, src, dst, other):
-        return pltpu.make_async_remote_copy(
-            src_ref=src,
-            dst_ref=dst,
-            send_sem=send_sem.at[i, slot],
-            recv_sem=recv_sem.at[i, slot],
-            device_id=other,
-            device_id_type=MESH,
-        )
-
-    def add(dst, one, other):
-        dst[...] = (one[...].astype(F32) + other[...].astype(F32)).astype(BF)
-
-    def own(i):
-        return pltpu.make_async_copy(grads[i].at[:, :, :, c], mine[i], own_sem.at[i])
-
-    def step_one(i):
-        return remote(i, 0, grads[i].at[:, :, :, 1 - c], sib[i], sibling)
-
-    def step_two(i):
-        return [
-            remote(i, 1, mine[i].at[1 - x, pl.ds(0, 2), 1 - y], diag[i].at[0], over_x),
-            remote(i, 2, mine[i].at[1 - x, pl.ds(2, 2), 1 - y], diag[i].at[1], over_y),
-        ]
-
-    def step_three(i):
-        return [
-            remote(i, 3, mine[i].at[1 - x, :, y], side[i].at[0], over_x),
-            remote(i, 4, mine[i].at[x, :, 1 - y], side[i].at[1], over_y),
-        ]
-
-    def step_four(i):
-        return [
-            remote(i, 4 + k, mine[i].at[x, lax.rem(z + k, 4), y], far[i].at[k - 1], lines[k - 1])
-            for k in (1, 2, 3)
-        ]
-
-    started = []
-
-    def start(copies):
-        for copy in copies:
-            copy.start()
-            started.append(copy)
-
-    for i in range(count):
-        own(i).start()
-        start([step_one(i)])
-    for turn in range(count + 3):
-        if turn < count:
-            i = turn
-            own(i).wait()
-            step_one(i).wait_recv()
-
-            def sweep(n, _, i=i):
-                part = (n // 8, lax.rem(n // 2, 4), lax.rem(n, 2))
-                add(mine[i].at[part], mine[i].at[part], sib[i].at[part])
-                return 0
-
-            lax.fori_loop(0, 16, sweep, 0)
-            start(step_two(i))
-        if 0 <= turn - 1 < count:
-            i = turn - 1
-            two = step_two(i)
-            for copy in two:
-                copy.wait()
-
-            def sweep(n, _, i=i):
-                low, high = (x, n, 1 - y), (1 - x, 2 + n, y)
-                add(mine[i].at[low], mine[i].at[low], diag[i].at[0, n])
-                add(mine[i].at[high], mine[i].at[high], diag[i].at[1, n])
-                return 0
-
-            lax.fori_loop(0, 2, sweep, 0)
-            start(step_three(i))
-        if 0 <= turn - 2 < count:
-            i = turn - 2
-            three = step_three(i)
-            for copy in three:
-                copy.wait()
-
-            def sweep(n, _, i=i):
-                part = mine[i].at[x, n, y]
-                both = side[i][0, n].astype(F32) + side[i][1, n].astype(F32)
-                part[...] = (part[...].astype(F32) + both).astype(BF)
-                return 0
-
-            lax.fori_loop(0, 4, sweep, 0)
-            start(step_four(i))
-        if 0 <= turn - 3 < count:
-            i = turn - 3
-            for copy in step_four(i):
-                copy.wait()
-            total = mine[i][x, z, y].astype(F32)
-            for k in range(3):
-                total = total + far[i][k].astype(F32)
-            totals[i][...] = total
-    for i in range(count):
-        step_one(i).wait_send()
-
-
-def scatter_all(grads, rows):
-    count = len(grads)
-    widths = [g.shape[-1] for g in grads]
-    grads = [g.reshape(2, 4, 2, 2, rows, w) for g, w in zip(grads, widths)]
-    return pl.pallas_call(
-        functools.partial(scatter_kernel, count),
-        out_shape=[jax.ShapeDtypeStruct((rows, w), F32) for w in widths],
-        in_specs=[anywhere()] * count,
-        out_specs=[in_vmem()] * count,
-        scratch_shapes=[pltpu.VMEM((2, 4, 2, rows, w), BF) for w in widths]
-        + [pltpu.VMEM((2, 4, 2, rows, w), BF) for w in widths]
-        + [pltpu.VMEM((2, 2, rows, w), BF) for w in widths]
-        + [pltpu.VMEM((2, 4, rows, w), BF) for w in widths]
-        + [pltpu.VMEM((3, rows, w), BF) for w in widths]
-        + [
-            pltpu.SemaphoreType.DMA((count,)),
-            pltpu.SemaphoreType.DMA((count, 8)),
-            pltpu.SemaphoreType.DMA((count, 8)),
-        ],
-        compiler_params=params(collective_id=1, has_side_effects=True),
-        name="scatter_grads",
-    )(*grads)
+def add_into(dst, other):
+    dst[...] = (dst[...].astype(F32) + other[...].astype(F32)).astype(BF)
 
 
 def project_kernel(mine_ref, other_ref, w_ref, bias_ref, q_ref, k_ref, v_ref):
@@ -517,7 +388,7 @@
     )(q, k, v, *wholes)
 
 
-def attend_back_kernel(q_ref, k_ref, v_ref, do_ref, o_ref, p_ref, dq_ref, dk_ref, dv_ref):
+def attend_back_pair(q_ref, k_ref, v_ref, do_ref, o_ref, p_ref, dq_ref, dk_ref, dv_ref):
     sides = half_lanes()
     q, k, v, do = q_ref[0], k_ref[0], v_ref[0], do_ref[0]
     prod = do.astype(F32) * o_ref[0]
@@ -538,25 +409,134 @@
     dv_ref[0] = grad_v.astype(BF)
 
 
-def attend_back(q, k, v, do, o, p):
+def attend_back_kernel(*refs):
+    ins, grads = refs[:6], refs[6:9]
+    outs, totals = refs[9:12], refs[12:15]
+    refs = refs[15:]
+    mine, sib, diag, side = refs[:3], refs[3:6], refs[6:9], refs[9:12]
+    own_sem, send_sem, recv_sem = refs[12:]
+    i = pl.program_id(0)
+    x, z, y, c = place()
+    lines, over_x, over_y, sibling = neighbours()
+    wires = Wires(send_sem, recv_sem)
+
+    def keep(n):
+        return pltpu.make_async_copy(grads[n].at[:, :, :, c], mine[n], own_sem.at[n])
+
+    def after_sibling(n):
+        keep(n).wait()
+        wires.arrive(5 * n, sib[n])
+
+        def sweep(m, _):
+            part = (m // 8, lax.rem(m // 2, 4), lax.rem(m, 2))
+            add_into(mine[n].at[part], sib[n].at[part])
+            return 0
+
+        lax.fori_loop(0, 16, sweep, 0)
+        wires.start(5 * n + 1, mine[n].at[1 - x, pl.ds(0, 2), 1 - y], diag[n].at[0], over_x)
+        wires.start(5 * n + 2, mine[n].at[1 - x, pl.ds(2, 2), 1 - y], diag[n].at[1], over_y)
+
+    def after_diagonal(n):
+        wires.arrive(5 * n + 1, diag[n].at[0])
+        wires.arrive(5 * n + 2, diag[n].at[1])
+
+        def sweep(m, _):
+            add_into(mine[n].at[x, m, 1 - y], diag[n].at[0, m])
+            add_into(mine[n].at[1 - x, 2 + m, y], diag[n].at[1, m])
+            return 0
+
+        lax.fori_loop(0, 2, sweep, 0)
+        wires.start(5 * n + 3, mine[n].at[1 - x, :, y], side[n].at[0], over_x)
+        wires.start(5 * n + 4, mine[n].at[x, :, 1 - y], side[n].at[1], over_y)
+
+    def after_sides(n):
+        wires.arrive(5 * n + 3, side[n].at[0])
+        wires.arrive(5 * n + 4, side[n].at[1])
+
+        def sweep(m, _):
+            both = side[n][0, m].astype(F32) + side[n][1, m].astype(F32)
+            totals[n][m] = (mine[n][x, m, y].astype(F32) + both).astype(BF)
+            return 0
+
+        lax.fori_loop(0, 4, sweep, 0)
+
+    @pl.when(i == 0)
+    def _():
+        greet()
+        for n in range(3):
+            keep(n).start()
+            wires.start(5 * n, grads[n].at[:, :, :, 1 - c], sib[n], sibling)
+
+    @pl.when(i == 1)
+    def _():
+        after_sibling(0)
+
+    @pl.when(i == 2)
+    def _():
+        after_sibling(1)
+        after_diagonal(0)
+        after_sibling(2)
+
+    @pl.when(i == 4)
+    def _():
+        after_diagonal(1)
+        after_diagonal(2)
+
+    attend_back_pair(*ins, *outs)
+
+    @pl.when(i == pl.num_programs(0) - 1)
+    def _():
+        for n in range(3):
+            after_sides(n)
+        for n in range(3):
+            wires.sent(5 * n, grads[n].at[:, :, :, 1 - c])
+            wires.sent(5 * n + 1, mine[n].at[1 - x, pl.ds(0, 2), 1 - y])
+            wires.sent(5 * n + 2, mine[n].at[1 - x, pl.ds(2, 2), 1 - y])
+            wires.sent(5 * n + 3, mine[n].at[1 - x, :, y])
+            wires.sent(5 * n + 4, mine[n].at[x, :, 1 - y])
+
+
+def attend_back(q, k, v, do, o, p, grads, own_rows):
     _, rows, half = q.shape
     keys = k.shape[1]
     per = half // PAIR
     of_q = pl.BlockSpec((1, rows, PAIR), lambda i: (i // per, 0, lax.rem(i, per)))
     of_k = pl.BlockSpec((1, keys, PAIR), lambda i: (i // per, 0, lax.rem(i, per)))
+    of_p = pl.BlockSpec((2, rows, keys), lambda i: (i, 0, 0))
+    shapes = [
+        jax.ShapeDtypeStruct(q.shape, BF),
+        jax.ShapeDtypeStruct(k.shape, BF),
+        jax.ShapeDtypeStruct(k.shape, BF),
+    ]
+    common = dict(grid=(2 * per,), name="attend_back")
+    if not grads:
+        return pl.pallas_call(
+            attend_back_pair,
+            in_specs=[of_q, of_k, of_k, of_q, of_q, of_p],
+            out_specs=[of_q, of_k, of_k],
+            out_shape=shapes,
+            compiler_params=params(),
+            **common,
+        )(q, k, v, do, o, p)
+    widths = [g.shape[-1] for g in grads]
+    lined = [(4, own_rows, w) for w in widths]
     return pl.pallas_call(
         attend_back_kernel,
-        grid=(2 * per,),
-        in_specs=[of_q, of_k, of_k, of_q, of_q, pl.BlockSpec((2, rows, keys), lambda i: (i, 0, 0))],
-        out_specs=[of_q, of_k, of_k],
-        out_shape=[
-            jax.ShapeDtypeStruct(q.shape, BF),
-            jax.ShapeDtypeStruct(k.shape, BF),
-            jax.ShapeDtypeStruct(k.shape, BF),
+        in_specs=[of_q, of_k, of_k, of_q, of_q, of_p, *[anywhere()] * 3],
+        out_specs=[of_q, of_k, of_k, *[pl.BlockSpec(t, lambda i: (0, 0, 0)) for t in lined]],
+        out_shape=[*shapes, *[jax.ShapeDtypeStruct(t, BF) for t in lined]],
+        scratch_shapes=[
+            *[pltpu.VMEM((2, 4, 2, own_rows, w), BF) for w in widths],
+            *[pltpu.VMEM((2, 4, 2, own_rows, w), BF) for w in widths],
+            *[pltpu.VMEM((2, 2, own_rows, w), BF) for w in widths],
+            *[pltpu.VMEM((2, 4, own_rows, w), BF) for w in widths],
+            pltpu.SemaphoreType.DMA((3,)),
+            pltpu.SemaphoreType.DMA((15,)),
+            pltpu.SemaphoreType.DMA((15,)),
         ],
-        compiler_params=params(),
-        name="attend_back",
-    )(q, k, v, do, o, p)
+        compiler_params=params(collective_id=3, has_side_effects=True),
+        **common,
+    )(q, k, v, do, o, p, *[g.reshape(2, 4, 2, 2, own_rows, w) for g, w in zip(grads, widths)])
 
 
 def normal_parts(h):
@@ -749,6 +729,254 @@
     )(mine, other, dq, dk, dv, weight)
 
 
+def last_kernel(*refs):
+    a_ref, b_ref, dq_ref, dk_ref, dv_ref, w_ref, patch_ref, mask_ref, token_ref, vec_ref, dx1_ref = refs[:11]
+    lined = refs[11:14]
+    pg_ref, gv_ref, *totals = refs[14:20]
+    refs = refs[20:]
+    gw, sib, diag, side, da_ref, send_ref, landing = refs[:7]
+    far = refs[7:11]
+    send_sem, recv_sem = refs[11:]
+    x, z, y, c = place()
+    lines, over_x, over_y, sibling = neighbours()
+    wires = Wires(send_sem, recv_sem)
+    rows, depth = a_ref.shape
+    half = w_ref.shape[2] // 3
+    cut = rows // 32 * 16
+    spans = (pl.ds(0, cut), pl.ds(cut, rows - cut))
+    greet()
+
+    def along(n, source):
+        for k in (1, 2, 3):
+            wires.start(3 * n + k - 1, source(lax.rem(z + k, 4)), far[n].at[k - 1], lines[k - 1])
+
+    def settle(n, own):
+        total = own.astype(F32)
+        for k in range(3):
+            wires.arrive(3 * n + k, far[n].at[k])
+            total = total + far[n][k].astype(F32)
+        totals[n][...] = total
+
+    for n in range(3):
+        along(n + 1, lambda t, n=n: lined[n].at[t])
+    w = [[w_ref[h, :, n * half : (n + 1) * half] for n in range(3)] for h in range(2)]
+    for n, (start, size) in enumerate(((rows, cut), (rows + cut, rows - cut))):
+        span = pl.ds(start, size)
+        send = None
+        for h in range(2):
+            part = dot(dk_ref[h, span], w[h][1], NT) + dot(dv_ref[h, span], w[h][2], NT)
+            send = part if send is None else send + part
+        send_ref[spans[n]] = send.astype(BF)
+        wires.start(12 + n, send_ref.at[spans[n]], landing.at[spans[n]], over_x)
+    a, b = a_ref[...], b_ref[...]
+    own, other = pl.ds(0, rows), pl.ds(rows, rows)
+    for h in range(2):
+        for n in range(3):
+            if n == 0:
+                grad = dot(a, dq_ref[h], TN)
+            else:
+                ref = dk_ref if n == 1 else dv_ref
+                grad = dot(a, ref[h, own], TN) + dot(b, ref[h, other], TN)
+            gw[h, :, :, :, :, n * half : (n + 1) * half] = grad.astype(BF).reshape(4, 2, 2, -1, half)
+        wires.start(14 + h, gw.at[h, :, :, 1 - c], sib.at[h], sibling)
+    da = None
+    for h in range(2):
+        part = dot(dq_ref[h], w[h][0], NT) + dot(dk_ref[h, own], w[h][1], NT) + dot(dv_ref[h, own], w[h][2], NT)
+        da = part if da is None else da + part
+    da_ref[...] = da
+    for h in range(2):
+        wires.arrive(14 + h, sib.at[h])
+
+    def sweep(m, _):
+        i, j, k = m // 8, lax.rem(m // 2, 4), lax.rem(m, 2)
+        add_into(gw.at[i, j, k, c], sib.at[i, j, k])
+        return 0
+
+    lax.fori_loop(0, 16, sweep, 0)
+    wires.start(16, gw.at[1 - x, :, 1 - y, c], diag, over_y)
+    wires.start(18, gw.at[x, :, 1 - y, c], side.at[1], over_y)
+    gv_ref[...] = jnp.zeros_like(gv_ref)
+    for h in range(2):
+        cols = slice(h * half, (h + 1) * half)
+        gv_ref[2:3, cols] = jnp.sum(dq_ref[h].astype(F32), axis=0, keepdims=True)
+        gv_ref[3:4, cols] = jnp.sum(dv_ref[h].astype(F32), axis=0, keepdims=True)
+    tubes = jnp.where(mask_ref[...] > 0, token_ref[...], patch_ref[...].astype(F32))
+    centred = tubes - mean_rows(tubes)
+    scale = lax.rsqrt(mean_rows(centred * centred) + 1e-6)
+    xh = centred * scale
+    wires.arrive(16, diag)
+
+    def sweep_two(m, _):
+        add_into(gw.at[1 - x, m, y, c], diag.at[m])
+        return 0
+
+    lax.fori_loop(0, 4, sweep_two, 0)
+    wires.start(17, gw.at[1 - x, :, y, c], side.at[0], over_x)
+    for n in range(3):
+        settle(n + 1, lined[n][z])
+    for n in range(2):
+        wires.arrive(12 + n, landing.at[spans[n]])
+    da = da_ref[...] + landing[...].astype(F32)
+    gv_ref[0:1] = jnp.sum(da * xh, axis=0, keepdims=True)
+    gv_ref[1:2] = jnp.sum(da, axis=0, keepdims=True)
+    e = da * vec_ref[0:1]
+    dx = dx1_ref[...] + scale * (e - mean_rows(e) - xh * mean_rows(e * xh))
+    masked = mask_ref[...] > 0
+    pg_ref[...] = jnp.where(masked, 0.0, dx).astype(BF)
+    gv_ref[4:5] = jnp.sum(jnp.where(masked, dx, 0.0), axis=0, keepdims=True)
+    wires.arrive(17, side.at[0])
+    wires.arrive(18, side.at[1])
+
+    def sweep_three(m, _):
+        both = side[0, m].astype(F32) + side[1, m].astype(F32)
+        part = gw.at[x, m, y, c]
+        part[...] = (part[...].astype(F32) + both).astype(BF)
+        return 0
+
+    lax.fori_loop(0, 4, sweep_three, 0)
+    along(0, lambda t: gw.at[x, t, y, c])
+    settle(0, gw[x, z, y, c])
+    wires.drain()
+
+
+def last(a, b, dq, dk, dv, wa, patches, mask, token, vectors, dx1, lined):
+    rows, width = a.shape
+    own_rows = lined[0].shape[1]
+    widths = [wa.shape[2], *[t.shape[2] for t in lined]]
+    w = widths[0]
+    return pl.pallas_call(
+        last_kernel,
+        out_shape=[
+            jax.ShapeDtypeStruct((rows, width), BF),
+            jax.ShapeDtypeStruct((8, width), F32),
+            *[jax.ShapeDtypeStruct((own_rows, n), F32) for n in widths],
+        ],
+        in_specs=[in_vmem()] * 14,
+        out_specs=[in_vmem()] * 6,
+        scratch_shapes=[
+            pltpu.VMEM((2, 4, 2, 2, own_rows, w), BF),
+            pltpu.VMEM((2, 4, 2, own_rows, w), BF),
+            pltpu.VMEM((4, own_rows, w), BF),
+            pltpu.VMEM((2, 4, own_rows, w), BF),
+            pltpu.VMEM((rows, width), F32),
+            pltpu.VMEM((rows, width), BF),
+            pltpu.VMEM((rows, width), BF),
+            *[pltpu.VMEM((3, own_rows, n), BF) for n in widths],
+            pltpu.SemaphoreType.DMA((19,)),
+            pltpu.SemaphoreType.DMA((19,)),
+        ],
+        compiler_params=params(collective_id=1, has_side_effects=True),
+        name="last",
+    )(a, b, dq, dk, dv, wa, patches, mask, token, vectors, dx1, *lined)
+
+
+def lamb_kernel(*refs):
+    masters, firsts, seconds, totals = (refs[4 * n : 4 * n + 4] for n in range(4))
+    head_ref, tail_ref, hidden_ref, vec_ref, vfirst_ref, vsecond_ref = refs[16:22]
+    moments, squares, weights, copies = (refs[22 + 4 * n : 26 + 4 * n] for n in range(4))
+    token_ref, bias_ref, vm_ref, vs_ref, vw_ref, norm_ref = refs[38:44]
+    updates = refs[44:48]
+    held, came, final, send_sem, recv_sem = refs[48:]
+    x, z, y, c = place()
+    lines, over_x, over_y, sibling = neighbours()
+    wires = Wires(send_sem, recv_sem)
+    greet()
+    correct = 1.0 - 0.5**STEP
+
+    def terms(weight, moment, square, grad):
+        moment_new = 0.5 * moment + 0.5 * grad
+        square_new = 0.5 * square + 0.5 * grad * grad
+        update = moment_new / correct / (jnp.sqrt(square_new / correct) + 1e-06) + 0.01 * weight
+        return moment_new, square_new, update
+
+    def whole_sum(values):
+        return jnp.sum(jnp.sum(values, axis=0, keepdims=True), axis=1, keepdims=True)
+
+    lane = lax.broadcasted_iota(jnp.int32, (1, vec_ref.shape[1]), 1)
+    row = jnp.zeros((1, vec_ref.shape[1]), F32)
+    for n in range(4):
+        weight = masters[n][...]
+        moment, square, update = terms(weight, firsts[n][...], seconds[n][...], totals[n][...])
+        moments[n][...] = moment
+        squares[n][...] = square
+        updates[n][...] = update
+        row = jnp.where(lane == 2 * n, whole_sum(weight * weight), row)
+        row = jnp.where(lane == 2 * n + 1, whole_sum(update * update), row)
+    held[0, 0:4] = head_ref[0:4]
+    held[0, 4:7] = tail_ref[0:3]
+    held[0, 7:11] = hidden_ref[...]
+    held[0, 11:12] = tail_ref[3:4]
+    held[0, 12:13] = head_ref[4:5]
+    held[0, 13:14] = row
+    held[0, 14:] = jnp.zeros((2, vec_ref.shape[1]), F32)
+    for n, other in enumerate((sibling, over_x, over_y)):
+        wires.start(n, held.at[n], came.at[n], other)
+        wires.arrive(n, came.at[n])
+        both = held[n] + came[n]
+        if n < 2:
+            held[n + 1] = both
+        else:
+            final[z] = both
+    for k in (1, 2, 3):
+        wires.start(2 + k, final.at[z], final.at[z], lines[k - 1])
+    for k in (1, 2, 3):
+        wires.arrive(2 + k, final.at[lax.rem(z + 4 - k, 4)])
+    total = final[0] + final[1] + final[2] + final[3]
+    norms = jnp.sqrt(total[13:14])
+    for n in range(4):
+        size, length = norms[:, 2 * n : 2 * n + 1], norms[:, 2 * n + 1 : 2 * n + 2]
+        norm_ref[n : n + 1, 0:1] = size
+        norm_ref[n : n + 1, 1:2] = length
+        renewed = masters[n][...] - 0.5 * size / (length + 1e-06) * updates[n][...]
+        weights[n][...] = renewed
+        copies[n][...] = renewed.astype(BF)
+    grad = total[0:12]
+    vectors = vec_ref[...]
+    moment, square, update = terms(vectors, vfirst_ref[...], vsecond_ref[...], grad)
+    vm_ref[...] = moment
+    vs_ref[...] = square
+    size = jnp.sqrt(jnp.sum(vectors * vectors, axis=-1, keepdims=True))
+    length = jnp.sqrt(jnp.sum(update * update, axis=-1, keepdims=True))
+    vw_ref[...] = vectors - 0.5 * size / (length + 1e-06) * update
+    token_ref[...] = total[12:13]
+    bias_ref[...] = total[11:12]
+    wires.drain()
+
+
+def lamb(masters, firsts, seconds, totals, head, tail, hidden, vectors, vfirst, vsecond):
+    full = [jax.ShapeDtypeStruct(m.shape, F32) for m in masters]
+    width = vectors.shape[1]
+    flat = jax.ShapeDtypeStruct((1, width), F32)
+    like = jax.ShapeDtypeStruct(vectors.shape, F32)
+    return pl.pallas_call(
+        lamb_kernel,
+        out_shape=[
+            *full,
+            *full,
+            *full,
+            *[jax.ShapeDtypeStruct(m.shape, BF) for m in masters],
+            flat,
+            flat,
+            like,
+            like,
+            like,
+            jax.ShapeDtypeStruct((4, 2), F32),
+        ],
+        in_specs=[in_vmem()] * 22,
+        out_specs=[in_vmem()] * 22,
+        scratch_shapes=[
+            *[pltpu.VMEM(m.shape, F32) for m in masters],
+            pltpu.VMEM((3, 16, width), F32),
+            pltpu.VMEM((3, 16, width), F32),
+            pltpu.VMEM((4, 16, width), F32),
+            pltpu.SemaphoreType.DMA((6,)),
+            pltpu.SemaphoreType.DMA((6,)),
+        ],
+        compiler_params=params(collective_id=4, has_side_effects=True),
+        name="lamb",
+    )(*masters, *firsts, *seconds, *totals, head, tail, hidden, vectors, vfirst, vsecond)
+
+
 def lamb_terms(weight, moment, square, gradient):
     moment_new = 0.5 * moment + 0.5 * gradient
     square_new = 0.5 * square + 0.5 * gradient * gradient
@@ -799,41 +1027,61 @@
         shrink_master,
     ]
     shards = [m.astype(BF) for m in masters]
-    swap = [(0, 1), (1, 0)]
     mask, token, dy = cube_mask.reshape(rows, 1), mask_token[None], cotangent[0]
-    chosen = mask > 0
-    x = jnp.where(chosen, token, patches[0].astype(F32))
-    centred = x - mean_rows(x)
-    scale = lax.rsqrt(mean_rows(centred * centred) + 1e-6)
+    firsts = [attend_first.reshape(own_rows, -1), mixing_first, expand_first, shrink_first]
+    seconds = [attend_second.reshape(own_rows, -1), mixing_second, expand_second, shrink_second]
     if direct:
         *wholes, q, k, v, a1, a1_other = first(shards, patches[0], mask, token, vectors)
         wa = wholes[0].reshape(2, width, -1)
         o, o_low, p, *rest = attend(q, k, v, wholes[1:])
         wm, we, ws = (w.reshape(2, width, -1) for w in rest)
-    else:
-        wa, wm, we, ws = (
-            lax.all_gather(lax.all_gather(s, "dp", axis=0, tiled=True), "mp", axis=0) for s in shards
+        block_out, dx1, do, gm, ge, gs, gu, gv = middle(
+            patches[0], mask, token, o_low, dy, vectors, wm, we, ws
         )
-        a1 = (centred * scale * vectors[0] + vectors[1]).astype(BF)
-        a1_other = lax.ppermute(a1, "mp", swap)
-        q, k, v = project(a1, a1_other, wa, vectors[2:4])
-        o, o_low, p = attend(q, k, v, [])
+        dq, dk, dv, ts, te, tm = attend_back(q, k, v, do, o, p, [gs, ge, gm], own_rows)
+        patch_grad, head, *totals = last(
+            a1, a1_other, dq, dk, dv, wa, patches[0], mask, token, vectors, dx1, [tm, te, ts]
+        )
+        done = lamb(
+            masters, firsts, seconds, totals, head, gv, gu.reshape(4, width), vectors, vector_first, vector_second
+        )
+        results = []
+        for n in range(4):
+            group = [done[n], done[4 + n], done[8 + n], done[12 + n]]
+            if n == 0:
+                group = [g.reshape(attend_master.shape) for g in group]
+            results.extend(group)
+        token_grad, bias_grad, *vector_results = done[16:]
+        return (
+            block_out[None],
+            patch_grad[None],
+            token_grad[0],
+            bias_grad[0],
+            *results,
+            *vector_results,
+        )
+    swap = [(0, 1), (1, 0)]
+    chosen = mask > 0
+    x = jnp.where(chosen, token, patches[0].astype(F32))
+    centred = x - mean_rows(x)
+    scale = lax.rsqrt(mean_rows(centred * centred) + 1e-6)
+    wa, wm, we, ws = (
+        lax.all_gather(lax.all_gather(s, "dp", axis=0, tiled=True), "mp", axis=0) for s in shards
+    )
+    a1 = (centred * scale * vectors[0] + vectors[1]).astype(BF)
+    a1_other = lax.ppermute(a1, "mp", swap)
+    q, k, v = project(a1, a1_other, wa, vectors[2:4])
+    o, o_low, p = attend(q, k, v, [])
     block_out, dx1, do, gm, ge, gs, gu, gv = middle(
         patches[0], mask, token, o_low, dy, vectors, wm, we, ws
     )
-    dq, dk, dv = attend_back(q, k, v, do, o, p)
+    dq, dk, dv = attend_back(q, k, v, do, o, p, [], own_rows)
     da1, da1_send, ga, gqv = unproject(a1, a1_other, dq, dk, dv, wa)
     da1 = da1 + lax.ppermute(da1_send, "mp", swap).astype(F32)
-    grads = [ga, gm, ge, gs]
-    if direct:
-        totals = scatter_all(grads, own_rows)
-    else:
-        totals = []
-        for g in grads:
-            g = lax.psum_scatter(g, "mp", scatter_dimension=0, tiled=True)
-            totals.append(
-                lax.psum_scatter(g[0].astype(F32), "dp", scatter_dimension=0, tiled=True)
-            )
+    totals = []
+    for g in (ga, gm, ge, gs):
+        g = lax.psum_scatter(g, "mp", scatter_dimension=0, tiled=True)
+        totals.append(lax.psum_scatter(g[0].astype(F32), "dp", scatter_dimension=0, tiled=True))
     xh = centred * scale
     e = da1 * vectors[0]
     dx = dx1 + scale * (e - mean_rows(e) - xh * mean_rows(e * xh))
@@ -850,15 +1098,7 @@
         ],
         axis=0,
     )
-    terms = [
-        lamb_terms(w, m, s, g)
-        for w, m, s, g in zip(
-            masters,
-            [attend_first.reshape(own_rows, -1), mixing_first, expand_first, shrink_first],
-            [attend_second.reshape(own_rows, -1), mixing_second, expand_second, shrink_second],
-            totals,
-        )
-    ]
+    terms = [lamb_terms(w, m, s, g) for w, m, s, g in zip(masters, firsts, seconds, totals)]
     squares = jnp.stack([t[3] for t in terms])
     vector_total, token_grad, square_total = lax.psum(
         (vector_part, token_part, squares), ("dp", "mp")

time: 416 us -> 336 us (0.81)
  blocking collectives: 42.1 us -> 0 us
  other arithmetic: 32.6 us -> 8.77 us
  Pallas kernels: 310 us -> 296 us
  local copies, waits for them, and re-layouts: 16.8 us -> 25.3 us
  between operations: 6.67 us -> 1.12 us
    psum x1 -> x0, blocking collectives: 42.1 us -> none  [per_device(): lax.psum((vector_part, token_part, squares), ('dp', 'mp'))]
    pallas_call x3, Pallas kernels: 153 us -> 138 us  [the longest x1 60.9 us: attend_back(): pl.pallas_call(attend_back_kernel, in_specs=[of_q, of_k, of_k, of_q, of_q...]
    reduce_sum x9 -> x0, other arithmetic: 13.5 us -> none  [the longest x3 5.77 us: lamb_terms(): jnp.sum(weight * weight)]
    unnamed x72 -> x60, local copies, waits for them, and re-layouts: 3.03 us -> 15.7 us
    another operation x4 -> x0, other arithmetic: 5.98 us -> none  [per_device(): squares = jnp.stack([t[3] for t in terms])]
  transfers between devices with their start and end apart: 1 -> 0, of which waited for: 0 -> 0; matrix products, arithmetic and copies ran while one was open for 5% -> 0% of each run, Pallas kernels for 22% -> 0%
where the time goes in v3:
time: 336 us; the launch traced here: 331 us
  Pallas kernels  296 us (88%)
  local copies, waits for them, and re-layouts  25.3 us (8%)
  other arithmetic  8.77 us (3%)
    pallas_call x1, Pallas kernels, attend_back(): pl.pallas_call(attend_back_kernel, in_specs=[of_q, of_k, of_k, of_q, of_q...  60.9 us
    pallas_call x1, Pallas kernels, last(): pl.pallas_call(last_kernel, out_shape=[jax.ShapeDtypeStruct((rows, width)...  58 us
    pallas_call x1, Pallas kernels, first(): pl.pallas_call(first_kernel, out_shape=[*wholes, jax.ShapeDtypeStruct((2,...  56.1 us
    pallas_call x1, Pallas kernels, attend(): pl.pallas_call(attend_kernel, in_specs=[of_q, of_k, of_k, *[anywhere()] *...  55.6 us
    pallas_call x1, Pallas kernels, middle(): pl.pallas_call(middle_kernel, grid=(steps,), in_specs=[whole((rows, width...  45.5 us
    pallas_call x1, Pallas kernels, lamb(): pl.pallas_call(lamb_kernel, out_shape=[*full, *full, *full, *[jax.ShapeDt...  19.6 us
    unnamed x60, local copies, waits for them, and re-layouts  15.7 us

profile of v3, /device:TPU:0, one launch (start us, length us, event | category | flops | bytes accessed | tf_op | source)
XLA Modules:
  0.0 330.9 jit_solution(15132669187330522779)
XLA Ops:
  0.7 1.6 copy.56.refs_5_.mask_ref.refs_7_
  2.3 1.3 broadcast_in_dim.9.refs_6_.token_ref.refs_8_
  3.6 0.9 copy.69
  5.2 1.6 convert_element_type.14.refs_2_
  6.9 1.6 convert_element_type.15.refs_3_
  8.5 1.5 convert_element_type.13.refs_1_
  10.0 56.1 %first.1 = (bf16[2,4,2,2,48,1152]{5,4,3,2,1,0:T(8,128)(2,1)}, bf16[2,4,2,2,48,384]{5,4,3,2,1,0:T(8,128)(2,1)}, bf16[2,4,2,2,48,1536]{5,4,3,2,1,0:T(8,128)(2,1)},...) custom-call(bf16[48,1152]{1,0:T(8,128)(2,1)} %convert_element_type.1, ...), custom_call_target="tpu_custom_call" | custom-call | tf_op jit(solution)/shard_map/first/pallas_call | solution.py:216
  66.1 55.6 %attend.1 = (f32[2,784,384]{2,1,0:T(8,128)}, bf16[2,784,384]{2,1,0:T(8,128)(2,1)}, bf16[12,784,1568]{2,1,0:T(8,128)(2,1)}, bf16[2,4,2,2,48,384]{5,4,3,2,1,0:T(8,...) custom-call(bf16[2,784,384]{2,1,0:T(8,128)(2,1)} %get-tuple-element., ...), custom_call_target="tpu_custom_call", output_to_operand_aliasing={{3}: (3, {}), {4}: (4, {}), {5}: (5, {})} | custom-call | tf_op jit(solution)/shard_map/attend/pallas_call | solution.py:379
  121.8 0.8 slice_bitcast_fusion
  123.2 45.5 %middle.1 = (bf16[784,768]{1,0:T(8,128)(2,1)}, f32[784,768]{1,0:T(8,128)}, bf16[2,784,384]{2,1,0:T(8,128)(2,1)}, bf16[2,768,384]{2,1,0:T(8,128)(2,1)}, bf16[2,76...) custom-call(bf16[784,768]{1,0:T(8,128)(2,1)} %bitcast.39, ...), custom_call_target="tpu_custom_call" | custom-call | tf_op jit(solution)/shard_map/middle/pallas_call | solution.py:644
  168.6 60.9 %attend_back.1 = (bf16[2,784,384]{2,1,0:T(8,128)(2,1)}, bf16[2,1568,384]{2,1,0:T(8,128)(2,1)}, bf16[2,1568,384]{2,1,0:T(8,128)(2,1)}, bf16[4,48,1536]{2,1,0:T(8,...) custom-call(bf16[2,784,384]{2,1,0:T(8,128)(2,1)} %get-tuple-element.81.refs_0_, ...), custom_call_target="tpu_custom_call" | custom-call | tf_op jit(solution)/shard_map/attend_back/pallas_call | solution.py:523
  229.6 58.0 %last.1 = (bf16[784,768]{1,0:T(8,128)(2,1)}, f32[8,768]{1,0:T(8,128)}, f32[48,1152]{1,0:T(8,128)}, f32[48,384]{1,0:T(8,128)}, f32[48,1536]{1,0:T(8,128)}, /*index=5*/f32[48,1536]{1,0:T(8,128)}) custom-call(bf16[784,768]{1,0:T(8,128)(2,1)} %get-tuple-element.92.refs_0_, bf16[784,768]{1,0:T(8,128)(2,1)} %get-tuple-element.93.refs_1_, ...), custom_call_target="tpu_custom_call" | custom-call | tf_op jit(solution)/shard_map/last/pallas_call | solution.py:847
  290.8 19.6 %lamb.1 = (f32[48,1152]{1,0:T(8,128)}, f32[48,384]{1,0:T(8,128)}, f32[48,1536]{1,0:T(8,128)}, f32[48,1536]{1,0:T(8,128)}, f32[48,1152]{1,0:T(8,128)}, /*index=5*...) custom-call(f32[48,1152]{1,0:T(8,128)} %bitcast.46, ...), custom_call_target="tpu_custom_call" | custom-call | tf_op jit(solution)/shard_map/lamb/pallas_call | solution.py:951
  310.5 1.9 copy_bitcast_fusion
  312.4 1.7 copy.77
  314.0 1.6 copy.78
  315.6 1.3 reduce.1
  316.9 1.3 reduce.2
  318.2 1.3 copy.64
  319.5 1.0 copy.98
  323.1 0.7 copy.103
  323.8 0.7 copy.104
  324.5 0.7 copy.105
  325.9 0.7 copy.107
  (58 shorter events, 11.7 us)
Async XLA Ops:
  4.5 117.2 %copy-start = (f32[3,6,8,384]{3,2,0,1:T(8,128)}, f32[3,6,8,384]{3,2,0,1:T(8,128)S(1)}, u32[]{:S(2)}) copy-start(f32[3,6,8,384]{3,2,0,1:T(8,128)S(1)} %copy.69) | copy-start | bytes 663556
  229.5 58.6 %copy-start.19 = (f32[1,3072]{1,0:T(1,128)S(1)}, f32[1,3072]{1,0:T(1,128)}, u32[]{:S(2)}) copy-start(f32[1,3072]{1,0:T(1,128)} %get-tuple-element.115) | copy-start | bytes 36868
  229.5 59.9 %copy-start.8 = (f32[48,3,384]{2,0,1:T(8,128)S(1)}, f32[48,3,384]{2,0,1:T(8,128)}, u32[]{:S(2)}) copy-start(f32[48,3,384]{2,0,1:T(8,128)} %param.27) | copy-start | bytes 663556
  229.5 60.6 %copy-start.9 = (f32[48,3,384]{2,0,1:T(8,128)S(1)}, f32[48,3,384]{2,0,1:T(8,128)}, u32[]{:S(2)}) copy-start(f32[48,3,384]{2,0,1:T(8,128)} %param.28) | copy-start | bytes 663556
  290.8 28.7 %copy-start.1 = (bf16[784,768]{1,0:T(8,128)(2,1)S(1)}, bf16[784,768]{1,0:T(8,128)(2,1)}, u32[]{:S(2)}) copy-start(bf16[784,768]{1,0:T(8,128)(2,1)} %get-tuple-element.108) | copy-start | bytes 3612676
  310.4 10.1 %copy-start.14 = (f32[48,384]{1,0:T(8,128)S(1)}, f32[48,384]{1,0:T(8,128)}, u32[]{:S(2)}) copy-start(f32[48,384]{1,0:T(8,128)} %get-tuple-element.220) | copy-start | bytes 221188
  310.4 10.8 %copy-start.13 = (f32[48,384]{1,0:T(8,128)S(1)}, f32[48,384]{1,0:T(8,128)}, u32[]{:S(2)}) copy-start(f32[48,384]{1,0:T(8,128)} %get-tuple-element.221) | copy-start | bytes 221188
  310.4 11.4 %copy-start.12 = (f32[48,384]{1,0:T(8,128)S(1)}, f32[48,384]{1,0:T(8,128)}, u32[]{:S(2)}) copy-start(f32[48,384]{1,0:T(8,128)} %get-tuple-element.222) | copy-start | bytes 221188
  310.4 12.1 %copy-start.18 = (bf16[48,384]{1,0:T(8,128)(2,1)S(1)}, bf16[48,384]{1,0:T(8,128)(2,1)}, u32[]{:S(2)}) copy-start(bf16[48,384]{1,0:T(8,128)(2,1)} %get-tuple-element.223) | copy-start | bytes 110596
  310.4 12.7 %copy-start.7 = (f32[48,1536]{1,0:T(8,128)S(1)}, f32[48,1536]{1,0:T(8,128)}, u32[]{:S(2)}) copy-start(f32[48,1536]{1,0:T(8,128)} %get-tuple-element.224) | copy-start | bytes 884740
  310.4 13.4 %copy-start.6 = (f32[48,1536]{1,0:T(8,128)S(1)}, f32[48,1536]{1,0:T(8,128)}, u32[]{:S(2)}) copy-start(f32[48,1536]{1,0:T(8,128)} %get-tuple-element.225) | copy-start | bytes 884740
  312.4 12.2 %copy-start.5 = (f32[48,1536]{1,0:T(8,128)S(1)}, f32[48,1536]{1,0:T(8,128)}, u32[]{:S(2)}) copy-start(f32[48,1536]{1,0:T(8,128)} %get-tuple-element.226) | copy-start | bytes 884740
  315.6 9.6 %copy-start.11 = (bf16[48,1536]{1,0:T(8,128)(2,1)S(1)}, bf16[48,1536]{1,0:T(8,128)(2,1)}, u32[]{:S(2)}) copy-start(bf16[48,1536]{1,0:T(8,128)(2,1)} %get-tuple-element.227) | copy-start | bytes 442372
  319.5 6.4 %copy-start.4 = (f32[48,1536]{1,0:T(8,128)S(1)}, f32[48,1536]{1,0:T(8,128)}, u32[]{:S(2)}) copy-start(f32[48,1536]{1,0:T(8,128)} %get-tuple-element.228) | copy-start | bytes 884740
  319.5 7.1 %copy-start.3 = (f32[48,1536]{1,0:T(8,128)S(1)}, f32[48,1536]{1,0:T(8,128)}, u32[]{:S(2)}) copy-start(f32[48,1536]{1,0:T(8,128)} %get-tuple-element.229) | copy-start | bytes 884740
  320.5 6.8 %copy-start.2 = (f32[48,1536]{1,0:T(8,128)S(1)}, f32[48,1536]{1,0:T(8,128)}, u32[]{:S(2)}) copy-start(f32[48,1536]{1,0:T(8,128)} %get-tuple-element.230) | copy-start | bytes 884740
  320.5 7.5 %copy-start.10 = (bf16[48,1536]{1,0:T(8,128)(2,1)S(1)}, bf16[48,1536]{1,0:T(8,128)(2,1)}, u32[]{:S(2)}) copy-start(bf16[48,1536]{1,0:T(8,128)(2,1)} %get-tuple-element.231) | copy-start | bytes 442372
  320.5 8.2 %copy-start.17 = (f32[12,768]{1,0:T(8,128)S(1)}, f32[12,768]{1,0:T(8,128)}, u32[]{:S(2)}) copy-start(f32[12,768]{1,0:T(8,128)} %get-tuple-element.232) | copy-start | bytes 110596
  320.5 8.8 %copy-start.16 = (f32[12,768]{1,0:T(8,128)S(1)}, f32[12,768]{1,0:T(8,128)}, u32[]{:S(2)}) copy-start(f32[12,768]{1,0:T(8,128)} %get-tuple-element.233) | copy-start | bytes 110596
  320.6 9.4 %copy-start.15 = (f32[12,768]{1,0:T(8,128)S(1)}, f32[12,768]{1,0:T(8,128)}, u32[]{:S(2)}) copy-start(f32[12,768]{1,0:T(8,128)} %get-tuple-element.234) | copy-start | bytes 110596
